TPU v7x, 512 devices: a whole 4x4x16 slice. The times are simulated.
512 devices in a mesh: slide: 16 (over y, x_lo, core), row: 32 (over z, x_hi).
Axes of the slice: x: 4 (x_hi: 2, x_lo: 2; x = x_hi * 2 + x_lo), y: 4, z: 16, core: 2. Of those that a mesh axis runs over, the one named last changes fastest.
Arguments:
- trunk_c3: bfloat16 [16, 256, 32, 512], P('slide', 'row'), may hold values from -6 to 6
- trunk_c4: bfloat16 [16, 128, 16, 1024], P('slide', 'row'), may hold values from -6 to 6
- feat_p3: bfloat16 [16, 256, 32, 256], P('slide', 'row'), may hold values from -6 to 6
- feat_p4: bfloat16 [16, 128, 16, 256], P('slide', 'row'), may hold values from -6 to 6
- pre_p3: bfloat16 [16, 256, 32, 256], P('slide', 'row'), may hold values from -6 to 6
- pre_p4: bfloat16 [16, 128, 16, 256], P('slide', 'row'), may hold values from -6 to 6
- grad_p3: bfloat16 [16, 256, 32, 256], P('slide', 'row'), may hold values from -6 to 6
- grad_p4: bfloat16 [16, 128, 16, 256], P('slide', 'row'), may hold values from -6 to 6
- keep_p3: int32 [16, 256, 32], P('slide', 'row'), may hold values 0 or 1
- keep_p4: int32 [16, 128, 16], P('slide', 'row'), may hold values 0 or 1
- head_w: bfloat16 [9, 256, 256], replicated, may hold values from -0.125 to 0.125
- lateral_c3: bfloat16 [512, 256], replicated, may hold values from -0.25 to 0.25
- lateral_c4: bfloat16 [1024, 256], replicated, may hold values from -0.1875 to 0.1875
Outputs:
- trunk_c3_grad: bfloat16 [16, 256, 32, 512], P('slide', 'row')
- trunk_c4_grad: bfloat16 [16, 128, 16, 1024], P('slide', 'row')
- head_grad: float32 [2304, 256], P('row')
- bias_grad: float32 [256], P('row')
- lateral_c3_grad: float32 [512, 256], P('row')
- lateral_c4_grad: float32 [1024, 256], P('row')
All inputs are finite; a program needn't handle non-finite values. No bound on the sum of `keep_p3` or of `keep_p4` on one device may be relied on, other than what follows from the above.
Results may differ from a plain program's by a relative error of at most 0.011.
Values may be sent and summed in bfloat16 or wider, within the bound.
A program may use at most 64 MiB of HBM per device.

v0:
```python
import jax
import jax.numpy as jnp
from jax import lax
from jax.sharding import PartitionSpec as P

loss_scale = 256.0


def extended_2(cells, sides, width):
    for axis, dim in sides:
        count = lax.axis_size(axis)
        ends = count - 1
        head = lax.slice_in_dim(cells, 0, width, axis=dim)
        tail = lax.slice_in_dim(cells, cells.shape[dim] - width, cells.shape[dim], axis=dim)
        cells = jnp.concatenate(
            [
                lax.ppermute(tail, axis, [(i, (i + 1) % count) for i in range(ends)]),
                cells,
                lax.ppermute(head, axis, [((i + 1) % count, i) for i in range(ends)]),
            ],
            axis=dim,
        )
    return cells


def tap_patches(extended, row_total, col_total, mirror):
    columns = []
    for row_tap in range(3):
        for col_tap in range(3):
            top_start = 2 - row_tap if mirror else row_tap
            left_start = 2 - col_tap if mirror else col_tap
            window = extended[
                top_start : top_start + row_total, left_start : left_start + col_total
            ]
            columns.append(window.reshape(row_total * col_total, extended.shape[-1]))
    return jnp.concatenate(columns, axis=1)


def widen_cols(block):
    return jnp.pad(block, ((0, 0), (1, 1), (0, 0)))


def contract_rows(left_side, right_side):
    return lax.dot_general(
        left_side, right_side, (((0,), (0,)), ((), ())), preferred_element_type=jnp.float32
    )


def level_back(feature, preact, cotangent, keep_mask, head_w, level_id):
    row_total, col_total, channels = (feature.shape[1], feature.shape[2], feature.shape[3])
    live = jnp.logical_and(keep_mask[..., None] == 1, preact > 0)
    delta = jnp.where(live, cotangent, jnp.zeros_like(cotangent))
    delta_flat = delta[0].reshape(row_total * col_total, channels)
    joined = jnp.concatenate((feature, delta), axis=3)
    if level_id == 3:
        extended = extended_2(joined, (("row", 1),), 1)
    else:
        extended = extended_2(joined, (("row", 1),), 1)
    extended = widen_cols(extended[0])
    delta_patches = tap_patches(extended[..., channels:], row_total, col_total, True)
    feat_patches = tap_patches(extended[..., :channels], row_total, col_total, False)
    weight_sum = contract_rows(feat_patches, delta_flat)
    flipped = head_w.transpose(0, 2, 1).reshape(9 * channels, channels)
    backward = jnp.dot(delta_patches, flipped, preferred_element_type=jnp.float32)
    bias_sum = jnp.sum(delta_flat.astype(jnp.float32), axis=0)
    return (backward, weight_sum, bias_sum)


def local(
    trunk_c3,
    trunk_c4,
    feat_p3,
    feat_p4,
    pre_p3,
    pre_p4,
    grad_p3,
    grad_p4,
    keep_p3,
    keep_p4,
    head_w,
    lateral_c3,
    lateral_c4,
):
    channels = head_w.shape[1]
    back_fine, wsum_fine, bsum_fine = level_back(feat_p3, pre_p3, grad_p3, keep_p3, head_w, 3)
    back_coarse, wsum_coarse, bsum_coarse = level_back(feat_p4, pre_p4, grad_p4, keep_p4, head_w, 4)
    fine_rows, fine_cols = (feat_p3.shape[1], feat_p3.shape[2])
    pooled = (
        back_fine.reshape(fine_rows // 2, 2, fine_cols // 2, 2, channels)
        .sum(axis=(1, 3))
        .reshape(-1, channels)
    )
    lat_fine = back_fine.astype(jnp.bfloat16)
    lat_coarse = (back_coarse + pooled).astype(jnp.bfloat16)
    trunk_fine = trunk_c3[0].reshape(-1, trunk_c3.shape[-1])
    trunk_coarse = trunk_c4[0].reshape(-1, trunk_c4.shape[-1])
    fine_lateral = contract_rows(trunk_fine, lat_fine)
    coarse_lateral = contract_rows(trunk_coarse, lat_coarse)
    partial_head = wsum_fine + wsum_coarse
    partial_bias = bsum_fine + bsum_coarse
    totals = lax.psum((partial_head, fine_lateral, coarse_lateral, partial_bias), ("slide", "row"))
    row_index = lax.axis_index("row")
    row_count = lax.axis_size("row")
    shares = tuple(
        (
            lax.dynamic_slice_in_dim(
                member, row_index * (member.shape[0] // row_count), member.shape[0] // row_count, 0
            )
            for member in totals
        )
    )
    fine_grad = lax.dot_general(
        lat_fine, lateral_c3, (((1,), (1,)), ((), ())), preferred_element_type=jnp.float32
    )
    coarse_grad = lax.dot_general(
        lat_coarse, lateral_c4, (((1,), (1,)), ((), ())), preferred_element_type=jnp.float32
    )
    fine_grad = fine_grad.astype(jnp.bfloat16).reshape(1, fine_rows, fine_cols, trunk_c3.shape[-1])
    coarse_grad = coarse_grad.astype(jnp.bfloat16).reshape(
        1, fine_rows // 2, fine_cols // 2, trunk_c4.shape[-1]
    )
    head_grad = shares[0] / loss_scale
    lateral_c3_grad = shares[1] / loss_scale
    lateral_c4_grad = shares[2] / loss_scale
    bias_grad = shares[3] / loss_scale
    return (fine_grad, coarse_grad, head_grad, bias_grad, lateral_c3_grad, lateral_c4_grad)


def solution(mesh):
    in_specs = (
        P("slide", "row", None, None),
        P("slide", "row", None, None),
        P("slide", "row", None, None),
        P("slide", "row", None, None),
        P("slide", "row", None, None),
        P("slide", "row", None, None),
        P("slide", "row", None, None),
        P("slide", "row", None, None),
        P("slide", "row", None),
        P("slide", "row", None),
        P(),
        P(),
        P(),
    )
    out_specs = (
        P("slide", "row", None, None),
        P("slide", "row", None, None),
        P("row", None),
        P("row"),
        P("row", None),
        P("row", None),
    )
    return jax.shard_map(local, mesh=mesh, in_specs=in_specs, out_specs=out_specs, check_vma=False)
```

profile of v0, /device:TPU:1, one launch (start us, length us, event | category | flops | bytes accessed | tf_op | source)
XLA Modules:
  0.0 553.8 jit_solution(1256241552961467269)
XLA Ops:
  7.2 0.7 compare_bitcast_fusion.1
  8.0 0.9 convert_reduce_fusion.1
  8.8 0.7 pad_maximum_fusion.3
  9.6 5.5 collective-permute-start.2
  15.0 1.3 collective-permute-start.3
  16.3 0.7 compare_bitcast_fusion
  17.0 1.1 convert_reduce_fusion
  18.1 0.7 pad_maximum_fusion.1
  18.9 5.5 collective-permute-start
  24.4 1.3 collective-permute-start.1
  25.7 1.6 copy.21
  27.7 0.6 copy-done.12
  28.4 2.2 collective-permute-done.1
  30.6 1.1 pad_slice_fusion
  31.9 0.5 fusion.3
  32.6 2.1 convolution_bitcast_fusion.1
  34.7 0.9 constant_dynamic-update-slice_fusion.25
  35.8 2.0 fusion.4
  37.8 0.2 reduce_sum.27
  38.0 1.4 fusion
  39.5 1.3 convolution_bitcast_fusion
  40.8 1.9 convolution_add_fusion
  42.7 114.1 %psum.29 = f32[256]{0:T(256)S(1)} all-reduce(f32[256]{0:T(256)S(1)} %add.36), channel_id=1, replica_groups=mesh['slide'=16,'row'=32] {'slide','row'}, use_global_device_ids=true, to_apply=%region_4.5 | all-reduce | flops 256 | bytes 2048 | tf_op jit(solution)/shard_map/psum | solution.py:101
  156.8 0.6 dynamic-slice_multiply_fusion.3
  157.4 0.9 convolution_convert_fusion.1
  158.3 1.0 convolution_convert_fusion
  159.3 382.7 %all-reduce.5.cloned.1.call-done = (f32[2304,256]{1,0:T(8,128)}, f32[512,256]{0,1:T(8,128)}, f32[1024,256]{0,1:T(8,128)}) async-done(((f32[2304,256]{1,0:T(8,128)}, f32[512,256]{0,1:T(8,128)}, f32[1024,256]{0,1:T(8,128)}), (f32[2304,256]{1,0:T(8,128)}, f32[512,256]{0,1:T(8,128)}, f32[1024,256]{0,1:T(8,128)})) %all-reduce.5.cloned.1.call-update) | async-done | bytes 3932176 | tf_op jit(solution)/shard_map/psum | solution.py:101
  542.0 1.0 dynamic-slice_multiply_fusion
  543.0 0.7 copy.23
  543.7 1.0 dynamic-slice_multiply_fusion.1
  544.7 0.7 copy.22
  545.4 1.5 dynamic-slice_multiply_fusion.2
  (80 shorter events, 0.8 us)
Async XLA Ops:
  7.2 150.2 %copy-start = (bf16[1024,256]{1,0:T(8,128)(2,1)S(1)}, bf16[1024,256]{1,0:T(8,128)(2,1)}, u32[]{:S(2)}) copy-start(bf16[1024,256]{1,0:T(8,128)(2,1)} %param.25) | copy-start | bytes 1572868
  7.2 534.9 %all-reduce.5.cloned.1.call-start = ((), (), s32[]{:S(2)}) async-start(), calls=%async_computation | async-start | bytes 7864320 | tf_op jit(solution)/shard_map/psum | solution.py:101
  8.8 18.5 %copy-start.2 = (bf16[1,4,16,256]{3,2,1,0:T(8,128)(2,1)}, bf16[1,4,16,256]{3,2,1,0:T(8,128)(2,1)S(1)}, u32[]{:S(2)}) copy-start(bf16[1,4,16,256]{3,2,1,0:T(8,128)(2,1)S(1)} %get-tuple-element.22) | copy-start | bytes 98308
  9.6 17.7 %collective-permute-start.2 = (bf16[1,1,16,512]{3,2,1,0:T(8,128)(2,1)S(1)}, bf16[1,1,16,512]{3,2,1,0:T(8,128)(2,1)S(1)}, u32[]{:S(2)}, u32[]{:S(2)}) collective-permute-start(bf16[1,1,16,512]{3,2,1,0:T(8,128)(2,1)S(1)} %get-tuple-element.63), channel_id=1, source_target_pairs={{0,1},{1,2},{2,3},{3,4},{4,5},{5,6},{6,7},{7,8},{8,9},{9,10},{10,1... | collective-permute-start | bytes 49160 | tf_op jit(solution)/shard_map/ppermute | solution.py:17
  15.0 12.2 %collective-permute-start.3 = (bf16[1,1,16,512]{3,2,1,0:T(8,128)(2,1)S(1)}, bf16[1,1,16,512]{3,2,1,0:T(8,128)(2,1)S(1)}, u32[]{:S(2)}, u32[]{:S(2)}) collective-permute-start(bf16[1,1,16,512]{3,2,1,0:T(8,128)(2,1)S(1)} %get-tuple-element.64), channel_id=1, source_target_pairs={{1,0},{2,1},{3,2},{4,3},{5,4},{6,5},{7,6},{8,7},{9,8},{10,9},{11,1... | collective-permute-start | bytes 49160 | tf_op jit(solution)/shard_map/ppermute | solution.py:19
  18.9 8.8 %collective-permute-start = (bf16[1,1,32,512]{3,2,1,0:T(8,128)(2,1)S(1)}, bf16[1,1,32,512]{3,2,1,0:T(8,128)(2,1)S(1)}, u32[]{:S(2)}, u32[]{:S(2)}) collective-permute-start(bf16[1,1,32,512]{3,2,1,0:T(8,128)(2,1)S(1)} %get-tuple-element.43), channel_id=1, source_target_pairs={{0,1},{1,2},{2,3},{3,4},{4,5},{5,6},{6,7},{7,8},{8,9},{9,10},{10,1... | collective-permute-start | bytes 98312 | tf_op jit(solution)/shard_map/ppermute | solution.py:17
  24.4 2.9 copy-start.17
  24.4 6.2 %collective-permute-start.1 = (bf16[1,1,32,512]{3,2,1,0:T(8,128)(2,1)S(1)}, bf16[1,1,32,512]{3,2,1,0:T(8,128)(2,1)S(1)}, u32[]{:S(2)}, u32[]{:S(2)}) collective-permute-start(bf16[1,1,32,512]{3,2,1,0:T(8,128)(2,1)S(1)} %get-tuple-element.44), channel_id=1, source_target_pairs={{1,0},{2,1},{3,2},{4,3},{5,4},{6,5},{7,6},{8,7},{9,8},{10,9},{11,1... | collective-permute-start | bytes 98312 | tf_op jit(solution)/shard_map/ppermute | solution.py:19
  27.3 3.3 copy-start.4
  27.5 0.7 copy-start.12
  27.6 0.7 copy-start.14
  32.5 3.1 copy-start.11
  32.5 3.1 copy-start.10
  32.6 3.1 copy-start.9
  32.6 3.2 copy-start.8
  32.6 3.2 copy-start.7
  32.6 3.2 copy-start.6
  34.7 1.1 copy-start.5
  37.8 1.7 copy-start.16
  38.0 2.8 copy-start.1
  38.0 2.8 copy-start.3
  38.0 2.8 copy-start.13
  42.7 115.6 %copy-start.15 = (bf16[512,256]{1,0:T(8,128)(2,1)S(1)}, bf16[512,256]{1,0:T(8,128)(2,1)}, u32[]{:S(2)}) copy-start(bf16[512,256]{1,0:T(8,128)(2,1)} %param.24) | copy-start | bytes 786436
Sparse Core Ops, SparseCore 0:
  42.8 499.1 all-reduce.4
where the time goes:
time: 555 us; the launch traced here: 554 us
  waiting for transfers between devices  385 us (69%)
  blocking collectives  114 us (21%)
  between operations  14.7 us (3%)
  starting transfers between devices  13.6 us (2%)
  matrix products  11.1 us (2%)
  other arithmetic  9.19 us (2%)
  local copies, waits for them, and re-layouts  6.28 us (1%)
    psum x1, waiting for transfers between devices, local(): lax.psum((partial_head, fine_lateral, coarse_lateral, partial_bias), ('sl...  383 us
    psum x1, blocking collectives, local(): lax.psum((partial_head, fine_lateral, coarse_lateral, partial_bias), ('sl...  114 us
  transfers between devices with their start and end apart: 5, of which 2 were waited for; matrix products, arithmetic and copies ran while one was open for 1% of the time, Pallas kernels for 0%

commit v1 on v0

v1 whole, which is shorter than its diff:
```python
import jax
import jax.numpy as jnp
from jax import lax
from jax.experimental import pallas as pl
from jax.experimental.pallas import tpu as pltpu
from jax.sharding import PartitionSpec as P

MESH = pl.DeviceIdType.MESH
F32 = jnp.float32
BF16 = jnp.bfloat16
LOSS_SCALE = 256.0

ROW_C3 = 2304
ROW_C4 = 2816
ROW_BIAS = 3840
ROWS = 3856
CORE_PARTS = ((768, 768), (0, 768), (1536, 768), (ROW_C3, 512), (ROW_C4, 1040))


def nt(a, b):
    return lax.dot_general(a, b, (((1,), (1,)), ((), ())), preferred_element_type=F32)


def nn(a, b):
    return jnp.dot(a, b, preferred_element_type=F32)


def kernel(
    tc3_h, tc4_h, f3_h, f4_h, p3_h, p4_h, g3_h, g4_h, k3_h, k4_h, hw_h, l3_h, l4_h,
    o_t3, o_t4, o_head, o_bias, o_l3, o_l4,
    tc3, tc4, f3, f4, p3, p4, g3, g4, k3, k4, hw, l3, l4,
    f3t, f4t, dx3, dx4, halo_s, halo_r, grads, core_s, core_r,
    bx, by, r1x, r1y, cx, cy, r2x, r2y, dz, r3, gath,
    in_sem, halo_ss, halo_rs, core_ss, core_rs, s1_ss, s1_rs, s2_ss, s2_rs,
    z_ss, z_rs, ag_ss, ag_rs, far_sem,
):
    slide = lax.axis_index("slide")
    row = lax.axis_index("row")
    core = lax.rem(slide, 2)
    x_lo = lax.rem(slide // 2, 2)
    y = slide // 4
    z = row // 2
    x_hi = lax.rem(row, 2)
    x = 2 * x_hi + x_lo

    def dev(xx, yy, zz, cc):
        return ((yy * 2 + lax.rem(xx, 2)) * 2 + cc, zz * 2 + xx // 2)

    sibling = (slide + 1 - 2 * core, row)
    above = (slide, lax.rem(row + 31, 32))
    below = (slide, lax.rem(row + 1, 32))
    x_dev = [dev(lax.rem(x + d, 4), y, z, core) for d in (1, 2, 3)]
    y_dev = [dev(x, lax.rem(y + d, 4), z, core) for d in (1, 2, 3)]

    def z_dev(d):
        return dev(x, y, lax.rem(z + d + 16, 16), core)

    pairs = [
        (k3_h, k3), (k4_h, k4), (p3_h, p3), (g3_h, g3), (p4_h, p4), (g4_h, g4), (f3_h, f3),
        (f4_h, f4), (hw_h, hw), (tc3_h, tc3), (tc4_h, tc4), (l3_h, l3), (l4_h, l4),
    ]
    loads = [pltpu.make_async_copy(a, b, in_sem.at[i]) for i, (a, b) in enumerate(pairs)]

    barrier = pltpu.get_barrier_semaphore()
    partners = [above, below, sibling] + x_dev + y_dev
    partners += [z_dev(d) for d in (-4, -3, -2, -1, 1, 2, 3, 4)]
    for who in partners:
        pl.semaphore_signal(barrier, inc=1, device_id=who, device_id_type=MESH)
    for ld in loads:
        ld.start()

    for ld in loads[:6]:
        ld.wait()

    def delta(keep, pre, grad, height, width):
        keep_t = jnp.transpose(keep[...].astype(F32))
        cols = [jnp.broadcast_to(keep_t[:, i : i + 1], (width, 256)) for i in range(height)]
        mask = jnp.concatenate(cols, axis=0)
        live = jnp.logical_and(mask > 0.5, pre[...].astype(F32) > 0.0)
        return jnp.where(live, grad[...].astype(F32), 0.0)

    def put_shifted(dst, start, rows, width, val):
        col = lax.rem(lax.broadcasted_iota(jnp.int32, (rows, 256), 0), width)
        ahead = jnp.where(col == width - 1, 0.0, pltpu.roll(val, rows - 1, 0))
        behind = jnp.where(col == 0, 0.0, pltpu.roll(val, 1, 0))
        dst[0, start : start + rows, :] = ahead.astype(BF16)
        dst[1, start : start + rows, :] = val.astype(BF16)
        dst[2, start : start + rows, :] = behind.astype(BF16)

    d3 = delta(k3, p3, g3, 8, 32)
    d4 = delta(k4, p4, g4, 4, 16)
    halo_s[0, 0:32, :] = d3[0:32].astype(BF16)
    halo_s[0, 32:48, :] = d4[0:16].astype(BF16)
    halo_s[1, 0:32, :] = d3[224:256].astype(BF16)
    halo_s[1, 32:48, :] = d4[48:64].astype(BF16)

    pl.semaphore_wait(barrier, len(partners))
    halos = []
    for i, who in enumerate((above, below)):
        cp = pltpu.make_async_remote_copy(
            src_ref=halo_s.at[i], dst_ref=halo_r.at[i], send_sem=halo_ss.at[i],
            recv_sem=halo_rs.at[i], device_id=who, device_id_type=MESH,
        )
        cp.start()
        halos.append(cp)
    for d in (-4, 4):
        pl.semaphore_signal(far_sem, inc=1, device_id=z_dev(d), device_id_type=MESH)

    put_shifted(dx3, 32, 256, 32, d3)
    put_shifted(dx4, 16, 64, 16, d4)

    ones = jnp.ones((16, 256), BF16)
    bias = nn(ones, dx3[1, 32:288, :]) + nn(ones[:, :64], dx4[1, 16:80, :])

    first = core == 0

    def emit(start, rows, val):
        lo, hi = val[:, :128], val[:, 128:]
        grads[start : start + rows, :] = jnp.where(first, lo, hi)
        core_s[start : start + rows, :] = jnp.where(first, hi, lo).astype(BF16)

    core_copies = []

    def send_core(i):
        start, rows = CORE_PARTS[i]
        cp = pltpu.make_async_remote_copy(
            src_ref=core_s.at[pl.ds(start, rows)], dst_ref=core_r.at[pl.ds(start, rows)],
            send_sem=core_ss.at[i], recv_sem=core_rs.at[i], device_id=sibling,
            device_id_type=MESH,
        )
        cp.start()
        core_copies.append(cp)

    emit(ROW_BIAS, 16, bias)
    loads[6].wait()
    loads[7].wait()
    f3t[...] = jnp.transpose(f3[...])
    f4t[...] = jnp.transpose(f4[...])

    def head_taps(a):
        for b in range(3):
            tap = 3 * a + b
            top3, top4 = (2 - a) * 32, (2 - a) * 16
            val = nn(f3t[...], dx3[b, top3 : top3 + 256, :])
            val = val + nn(f4t[...], dx4[b, top4 : top4 + 64, :])
            emit(tap * 256, 256, val)

    head_taps(1)
    send_core(0)
    for ld in loads[8:]:
        ld.wait()

    for cp in halos:
        cp.wait_recv()
    low = jnp.where(row < 31, halo_r[0].astype(F32), 0.0)
    top = jnp.where(row > 0, halo_r[1].astype(F32), 0.0)
    put_shifted(dx3, 0, 32, 32, top[0:32])
    put_shifted(dx3, 288, 32, 32, low[0:32])
    put_shifted(dx4, 0, 16, 16, top[32:48])
    put_shifted(dx4, 80, 16, 16, low[32:48])

    back = jnp.zeros((320, 256), F32)
    for a in range(3):
        for b in range(3):
            top3, top4 = (2 - a) * 32, (2 - a) * 16
            patch = jnp.concatenate(
                [dx3[b, top3 : top3 + 256, :], dx4[b, top4 : top4 + 64, :]], axis=0
            )
            back = back + nt(patch, hw[3 * a + b])
    back3 = back[0:256]
    back4 = back[256:320]
    lat3 = back3.astype(BF16)
    rest = (back3 - lat3.astype(F32)).astype(BF16)
    cell4 = lax.broadcasted_iota(jnp.int32, (64, 256), 0)
    cell3 = lax.broadcasted_iota(jnp.int32, (64, 256), 1)
    home = (cell3 // 64) * 16 + lax.rem(cell3, 32) // 2
    pool = jnp.where(home == cell4, 1.0, 0.0).astype(BF16)
    pooled = nn(pool, lat3) + nn(pool, rest)
    lat4 = (back4 + pooled).astype(BF16)

    head_taps(0)
    send_core(1)
    head_taps(2)
    send_core(2)
    emit(ROW_C3, 512, nn(jnp.transpose(tc3[...]), lat3))
    send_core(3)
    emit(ROW_C4, 1024, nn(jnp.transpose(tc4[...]), lat4))
    send_core(4)

    o_t3[...] = nt(lat3, l3[...]).astype(BF16)
    o_t4[...] = nt(lat4, l4[...]).astype(BF16)

    for i, (start, rows) in enumerate(CORE_PARTS):
        core_copies[i].wait_recv()
        grads[start : start + rows, :] += core_r[start : start + rows, :].astype(F32)

    def pack(dst, z_first, flip):
        def step(zz, carry):
            for xh in range(2):
                r = 2 * (zz + z_first) + xh
                base = pl.multiple_of(72 * r, 8)
                for blk in range(8):
                    if blk < 4:
                        val = grads[pl.ds(base + 16 * blk, 16), :]
                    elif blk == 4:
                        val = jnp.concatenate(
                            [grads[pl.ds(base + 64, 8), :], grads[ROW_BIAS : ROW_BIAS + 8, :]],
                            axis=0,
                        )
                    elif blk == 5:
                        val = grads[pl.ds(pl.multiple_of(ROW_C3 + 16 * r, 16), 16), :]
                    else:
                        at = ROW_C4 + 32 * r + 16 * (blk - 6)
                        val = grads[pl.ds(pl.multiple_of(at, 16), 16), :]
                    xx, yy = 2 * xh + blk % 2, blk // 2
                    if flip:
                        dst[yy, xx, zz] = val.astype(BF16)
                    else:
                        dst[xx, yy, zz] = val.astype(BF16)
            return carry

        lax.fori_loop(0, 8, step, 0)

    def exchange(src, at, dst, who, ss, rs, base):
        out = []
        for d in (2, 1, 3):
            cp = pltpu.make_async_remote_copy(
                src_ref=src.at[lax.rem(at + d, 4)], dst_ref=dst.at[d - 1],
                send_sem=ss.at[base + d - 1], recv_sem=rs.at[base + d - 1],
                device_id=who[d - 1], device_id_type=MESH,
            )
            cp.start()
            out.append(cp)
        return out

    sends = list(halos) + list(core_copies)
    pack(bx, 0, False)
    s1x = exchange(bx, x, r1x, x_dev, s1_ss, s1_rs, 0)
    pack(by, 8, True)
    s1y = exchange(by, y, r1y, y_dev, s1_ss, s1_rs, 3)

    def total(mine, got, i):
        acc = mine.astype(F32)
        for d in range(3):
            acc = acc + (got[d] if i is None else got[d, i]).astype(F32)
        return acc

    for cp in s1x:
        cp.wait_recv()
    for i in range(4):
        cx[i] = total(bx[x, i], r1x, i).astype(BF16)
    s2x = exchange(cx, y, r2x, y_dev, s2_ss, s2_rs, 0)
    for cp in s1y:
        cp.wait_recv()
    for i in range(4):
        cy[i] = total(by[y, i], r1y, i).astype(BF16)
    s2y = exchange(cy, x, r2y, x_dev, s2_ss, s2_rs, 3)

    def z_copy(piece, d):
        return pltpu.make_async_remote_copy(
            src_ref=dz.at[piece], dst_ref=r3.at[d], send_sem=z_ss.at[d], recv_sem=z_rs.at[d],
            device_id=z_dev(d), device_id_type=MESH,
        )

    def send_z(z_first):
        for piece in range(z_first, z_first + 8):
            d = lax.rem(piece - z + 16, 16)

            @pl.when(d != 0)
            def _():
                z_copy(piece, d).start()

    for cp in s2x:
        cp.wait_recv()
    dz[0:8] = total(cx[y], r2x, None).astype(BF16)
    pl.semaphore_wait(far_sem, 2)
    send_z(0)
    for cp in s2y:
        cp.wait_recv()
    dz[8:16] = total(cy[x], r2y, None).astype(BF16)
    send_z(8)

    acc = dz[z].astype(F32)
    for d in range(1, 16):
        z_copy(0, d).wait_recv()
        acc = acc + r3[d].astype(F32)

    gath[slide] = acc * (1.0 / LOSS_SCALE)
    gathers = []
    for o in range(1, 16):
        dy, dx, dc = o // 4, (o // 2) % 2, o % 2
        xl = lax.rem(x_lo + dx, 2)
        cc = lax.rem(core + dc, 2)
        cp = pltpu.make_async_remote_copy(
            src_ref=gath.at[slide], dst_ref=gath.at[slide], send_sem=ag_ss.at[o],
            recv_sem=ag_rs.at[o], device_id=dev(2 * x_hi + xl, lax.rem(y + dy, 4), z, cc),
            device_id_type=MESH,
        )
        cp.start()
        gathers.append(cp)
    for cp in gathers:
        cp.wait_recv()

    for c in range(2):
        lanes = slice(128 * c, 128 * c + 128)
        for blk in range(4):
            o_head[16 * blk : 16 * blk + 16, lanes] = gath[2 * blk + c]
        o_head[64:72, lanes] = gath[8 + c, 0:8, :]
        o_l3[:, lanes] = gath[10 + c]
        o_l4[0:16, lanes] = gath[12 + c]
        o_l4[16:32, lanes] = gath[14 + c]
    sums = jnp.concatenate([gath[8, 8:16, :], gath[9, 8:16, :]], axis=1)
    lane = lax.broadcasted_iota(jnp.int32, (8, 256), 1)
    sub = lax.broadcasted_iota(jnp.int32, (8, 256), 0)
    mine = jnp.where(lane == 8 * row + sub, sums, 0.0)
    for i in range(8):
        o_bias[i] = jnp.sum(mine[i : i + 1, :])

    for cp in sends + s1x + s1y + s2x + s2y + gathers:
        cp.wait_send()
    for d in range(1, 16):
        z_copy(0, d).wait_send()


def local(*args):
    shapes = (
        (256, 512), (64, 1024), (256, 256), (64, 256), (256, 256), (64, 256), (256, 256),
        (64, 256), (8, 32), (4, 16), (9, 256, 256), (512, 256), (1024, 256),
    )
    flat = [a.reshape(s) for a, s in zip(args, shapes)]
    vm = pltpu.VMEM
    dma = pltpu.SemaphoreType.DMA
    outs = pl.pallas_call(
        kernel,
        out_shape=(
            jax.ShapeDtypeStruct((256, 512), BF16),
            jax.ShapeDtypeStruct((64, 1024), BF16),
            jax.ShapeDtypeStruct((72, 256), F32),
            jax.ShapeDtypeStruct((8,), F32),
            jax.ShapeDtypeStruct((16, 256), F32),
            jax.ShapeDtypeStruct((32, 256), F32),
        ),
        in_specs=[pl.BlockSpec(memory_space=pl.ANY)] * 13,
        out_specs=(
            pl.BlockSpec(memory_space=vm), pl.BlockSpec(memory_space=vm),
            pl.BlockSpec(memory_space=vm), pl.BlockSpec(memory_space=pltpu.SMEM),
            pl.BlockSpec(memory_space=vm), pl.BlockSpec(memory_space=vm),
        ),
        scratch_shapes=[vm(a.shape, a.dtype) for a in flat] + [
            vm((256, 256), BF16), vm((256, 64), BF16),
            vm((3, 320, 256), BF16), vm((3, 96, 256), BF16),
            vm((2, 48, 256), BF16), vm((2, 48, 256), BF16),
            vm((ROWS, 128), F32), vm((ROWS, 128), BF16), vm((ROWS, 128), BF16),
            vm((4, 4, 8, 16, 128), BF16), vm((4, 4, 8, 16, 128), BF16),
            vm((3, 4, 8, 16, 128), BF16), vm((3, 4, 8, 16, 128), BF16),
            vm((4, 8, 16, 128), BF16), vm((4, 8, 16, 128), BF16),
            vm((3, 8, 16, 128), BF16), vm((3, 8, 16, 128), BF16),
            vm((16, 16, 128), BF16), vm((16, 16, 128), BF16), vm((16, 16, 128), F32),
            dma((13,)), dma((2,)), dma((2,)), dma((5,)), dma((5,)), dma((6,)), dma((6,)),
            dma((6,)), dma((6,)), dma((16,)), dma((16,)), dma((16,)), dma((16,)),
            pltpu.SemaphoreType.REGULAR,
        ],
        compiler_params=pltpu.CompilerParams(
            collective_id=0, has_side_effects=True, vmem_limit_bytes=56 << 20
        ),
        name="pyramid_backward",
    )(*flat)
    t3, t4, head, bias, lat3, lat4 = outs
    return (t3.reshape(1, 8, 32, 512), t4.reshape(1, 4, 16, 1024), head, bias, lat3, lat4)


def solution(mesh):
    big = P("slide", "row", None, None)
    in_specs = (big,) * 8 + (P("slide", "row", None),) * 2 + (P(),) * 3
    out_specs = (big, big, P("row", None), P("row"), P("row", None), P("row", None))
    return jax.shard_map(local, mesh=mesh, in_specs=in_specs, out_specs=out_specs, check_vma=False)
```

time: 555 us -> 59 us (0.11)
  waiting for transfers between devices: 385 us -> 0 us
  blocking collectives: 114 us -> 0 us
  Pallas kernels: 0 us -> 49.4 us
  between operations: 14.7 us -> 0.65 us
  starting transfers between devices: 13.6 us -> 0 us
  matrix products: 11.1 us -> 0 us
  other arithmetic: 9.19 us -> 0 us
    psum x1 -> x0, waiting for transfers between devices: 383 us -> none  [local(): lax.psum((partial_head, fine_lateral, coarse_lateral, partial_bias), ('sl...]
    psum x1 -> x0, blocking collectives: 114 us -> none  [local(): lax.psum((partial_head, fine_lateral, coarse_lateral, partial_bias), ('sl...]
    pallas_call x0 -> x1, Pallas kernels: none -> 49.4 us  [local(): pl.pallas_call(kernel, out_shape=(jax.ShapeDtypeStruct((256, 512), BF16),...]
    ppermute x4 -> x0, starting transfers between devices: 13.5 us -> none  [the longest x2 10.9 us: extended_2(): lax.ppermute(tail, axis, [(i, (i + 1) % count) for i in range(ends)])]
    dot_general x8 -> x0, matrix products: 11.1 us -> none  [the longest x4 7.26 us: contract_rows(): lax.dot_general(left_side, right_side, (((0,), (0,)), ((), ())), preferre...]
  transfers between devices with their start and end apart: 5 -> 0, of which waited for: 2 -> 0; matrix products, arithmetic and copies ran while one was open for 1% -> 0% of each run, Pallas kernels for 0% -> 0%
where the time goes in v1:
time: 59 us; the launch traced here: 58.6 us
  Pallas kernels  49.4 us (84%)
  local copies, waits for them, and re-layouts  8.56 us (15%)
  between operations  0.65 us (1%)
    pallas_call x1, Pallas kernels, local(): pl.pallas_call(kernel, out_shape=(jax.ShapeDtypeStruct((256, 512), BF16),...  49.4 us
    unnamed x6, local copies, waits for them, and re-layouts  8.56 us

profile of v1, /device:TPU:1, one launch (start us, length us, event | category | flops | bytes accessed | tf_op | source)
XLA Modules:
  0.0 58.6 jit_solution(13041547537455329256)
XLA Ops:
  0.6 49.4 %pyramid_backward.1 = (bf16[256,512]{1,0:T(8,128)(2,1)}, bf16[64,1024]{1,0:T(8,128)(2,1)}, f32[72,256]{1,0:T(8,128)}, f32[8]{0:T(128)}, f32[16,256]{1,0:T(8,128)}, /*index=5*/f32[32,256]{1,0:T(8,128)}) custom-call(bf16[256,512]{1,0:T(8,128)(2,1)} %bitcast.12, bf16[64,1024]{1,0:T(8,128)(2,1)} %bitcast.14, bf16[256,256]{1,0:T(8,128)(2,1)} %bitcast.15, ...), custom_call_target="tpu_custom_call" | custom-call | tf_op jit(solution)/shard_map/pyramid_backward/pallas_call | solution.py:333
  50.1 1.7 %copy.25 = bf16[1,8,32,512]{3,2,1,0:T(8,128)(2,1)} copy(bf16[1,8,32,512]{3,2,1,0:T(8,128)(2,1)} %bitcast.13) | data formatting | bytes 524288
  51.7 1.6 %copy.26 = bf16[1,4,16,1024]{3,2,1,0:T(8,128)(2,1)} copy(bf16[1,4,16,1024]{3,2,1,0:T(8,128)(2,1)} %bitcast.18) | data formatting | bytes 262144
  53.3 1.5 %copy.27 = f32[72,256]{1,0:T(8,128)} copy(f32[72,256]{1,0:T(8,128)} %get-tuple-element.26) | data formatting | bytes 147456
  54.8 1.1 %copy.28 = f32[8]{0:T(128)} copy(f32[8]{0:T(128)} %get-tuple-element.27) | data formatting | bytes 64
  55.9 1.3 %copy.29 = f32[16,256]{1,0:T(8,128)} copy(f32[16,256]{1,0:T(8,128)} %get-tuple-element.28) | data formatting | bytes 32768
  57.3 1.4 %copy.30 = f32[32,256]{1,0:T(8,128)} copy(f32[32,256]{1,0:T(8,128)} %get-tuple-element.29) | data formatting | bytes 65536

commit v2 on v1

v2 whole, which is shorter than its diff:
```python
import jax
import jax.numpy as jnp
from jax import lax
from jax.experimental import pallas as pl
from jax.experimental.pallas import tpu as pltpu
from jax.sharding import PartitionSpec as P

MESH = pl.DeviceIdType.MESH
F32 = jnp.float32
BF16 = jnp.bfloat16
LOSS_SCALE = 256.0

ROW_BIAS = 2304
ROW_C3 = 2320
ROW_C4 = 2832
ROWS = 3856
CORE_PARTS = ((768, 768), (0, 768), (1536, 784), (ROW_C3, 512), (ROW_C4, 1024))
EARLY, LATE = (0, 5), (5, 3)
Z_ORDER = (8, 7, 9, 6, 10, 5, 11, 4, 12, 3, 13, 2, 14, 1, 15)
SLIDE_ORDER = (11, 10, 9, 8, 7, 15, 6, 14, 5, 13, 4, 12, 3, 2, 1)


def nt(a, b):
    return lax.dot_general(a, b, (((1,), (1,)), ((), ())), preferred_element_type=F32)


def nn(a, b):
    return jnp.dot(a, b, preferred_element_type=F32)


def kernel(
    tc3_h, tc4_h, f3_h, f4_h, p3_h, p4_h, g3_h, g4_h, k3_h, k4_h, hw_h, l3_h, l4_h,
    t3, t4, gath,
    piece,
    tc3, tc4, f3, f4, p3, p4, g3, g4, k3, k4, hw, l3, l4,
    f3t, f4t, c3t, c4t, edge_t, dx3, dx4, halo_s, halo_r, part, back_s, early, grads,
    core_s, core_r, bx, by, r1x, r1y, cx, cy, r2x, r2y, dz, r3,
    in_sem, halo_ss, halo_rs, core_ss, core_rs, s1_ss, s1_rs, s2_ss, s2_rs,
    z_ss, z_rs, ag_ss, ag_rs, far_sem,
):
    slide = lax.axis_index("slide")
    row = lax.axis_index("row")
    core = lax.rem(slide, 2)
    x_lo = lax.rem(slide // 2, 2)
    y = slide // 4
    z = row // 2
    x_hi = lax.rem(row, 2)
    x = 2 * x_hi + x_lo

    def dev(xx, yy, zz, cc):
        return ((yy * 2 + lax.rem(xx, 2)) * 2 + cc, zz * 2 + xx // 2)

    sibling = (slide + 1 - 2 * core, row)
    above = (slide, lax.rem(row + 31, 32))
    below = (slide, lax.rem(row + 1, 32))
    x_dev = [dev(lax.rem(x + d, 4), y, z, core) for d in (1, 2, 3)]
    y_dev = [dev(x, lax.rem(y + d, 4), z, core) for d in (1, 2, 3)]

    def z_dev(d):
        return dev(x, y, lax.rem(z + d + 16, 16), core)

    pairs = [
        (p3_h, p3), (g3_h, g3), (k3_h, k3), (k4_h, k4), (p4_h, p4), (g4_h, g4), (f3_h, f3),
        (f4_h, f4), (hw_h, hw), (tc3_h, tc3), (tc4_h, tc4), (l3_h, l3), (l4_h, l4),
    ]
    loads = [pltpu.make_async_copy(a, b, in_sem.at[i]) for i, (a, b) in enumerate(pairs)]
    barrier = pltpu.get_barrier_semaphore()
    partners = [above, below]
    partners += [z_dev(d) for d in (-4, 4, -3, 3, -2, 2, -1, 1)] + x_dev + y_dev + [sibling]
    for ld in loads[:6]:
        ld.start()
    for who in partners:
        pl.semaphore_signal(barrier, inc=1, device_id=who, device_id_type=MESH)

    for ld in loads[:6]:
        ld.wait()
    for ld in loads[6:]:
        ld.start()

    def delta(keep, pre, grad, height, width):
        keep_t = jnp.transpose(keep[...].astype(F32))
        cols = [jnp.broadcast_to(keep_t[:, i : i + 1], (width, 256)) for i in range(height)]
        mask = jnp.concatenate(cols, axis=0)
        live = jnp.logical_and(mask > 0.5, pre[...].astype(F32) > 0.0)
        return jnp.where(live, grad[...].astype(F32), 0.0)

    def put_shifted(dst, start, rows, width, val):
        col = lax.rem(lax.broadcasted_iota(jnp.int32, (rows, 256), 0), width)
        ahead = jnp.where(col == width - 1, 0.0, pltpu.roll(val, rows - 1, 0))
        behind = jnp.where(col == 0, 0.0, pltpu.roll(val, 1, 0))
        dst[0, start : start + rows, :] = ahead.astype(BF16)
        dst[1, start : start + rows, :] = val.astype(BF16)
        dst[2, start : start + rows, :] = behind.astype(BF16)

    d3 = delta(k3, p3, g3, 8, 32)
    d4 = delta(k4, p4, g4, 4, 16)
    halo_s[0, 0:32, :] = d3[0:32].astype(BF16)
    halo_s[0, 32:48, :] = d4[0:16].astype(BF16)
    halo_s[1, 0:32, :] = d3[224:256].astype(BF16)
    halo_s[1, 32:48, :] = d4[48:64].astype(BF16)

    pl.semaphore_wait(barrier, len(partners))
    halos = []
    for i, who in enumerate((above, below)):
        cp = pltpu.make_async_remote_copy(
            src_ref=halo_s.at[i], dst_ref=halo_r.at[i], send_sem=halo_ss.at[i],
            recv_sem=halo_rs.at[i], device_id=who, device_id_type=MESH,
        )
        cp.start()
        halos.append(cp)
    for d in (-4, 4):
        pl.semaphore_signal(far_sem, inc=1, device_id=z_dev(d), device_id_type=MESH)

    put_shifted(dx3, 32, 256, 32, d3)
    put_shifted(dx4, 16, 64, 16, d4)
    for b in range(3):
        dx3[b, 0:32, :] = jnp.zeros((32, 256), BF16)
        dx3[b, 288:320, :] = jnp.zeros((32, 256), BF16)
        dx4[b, 0:16, :] = jnp.zeros((16, 256), BF16)
        dx4[b, 80:96, :] = jnp.zeros((16, 256), BF16)

    first = core == 0

    def emit(start, rows, val):
        lo, hi = val[:, :128], val[:, 128:]
        grads[start : start + rows, :] = jnp.where(first, lo, hi)
        core_s[start : start + rows, :] = jnp.where(first, hi, lo).astype(BF16)

    core_copies = []

    def send_core(i):
        start, rows = CORE_PARTS[i]
        cp = pltpu.make_async_remote_copy(
            src_ref=core_s.at[pl.ds(start, rows)], dst_ref=core_r.at[pl.ds(start, rows)],
            send_sem=core_ss.at[i], recv_sem=core_rs.at[i], device_id=sibling,
            device_id_type=MESH,
        )
        cp.start()
        core_copies.append(cp)

    ones = jnp.ones((16, 256), BF16)
    bias = nn(ones, dx3[1, 32:288, :]) + nn(ones[:, :64], dx4[1, 16:80, :])
    emit(ROW_BIAS, 16, bias)
    loads[6].wait()
    loads[7].wait()
    f3t[...] = jnp.transpose(f3[...])
    f4t[...] = jnp.transpose(f4[...])
    edge_t[0] = jnp.transpose(jnp.concatenate([f3[0:32, :], f4[0:16, :]], axis=0))
    edge_t[1] = jnp.transpose(jnp.concatenate([f3[224:256, :], f4[48:64, :]], axis=0))

    def tap_term(a, b):
        top3, top4 = (2 - a) * 32, (2 - a) * 16
        val = nn(f3t[...], dx3[b, top3 : top3 + 256, :])
        return val + nn(f4t[...], dx4[b, top4 : top4 + 64, :])

    for b in range(3):
        emit((3 + b) * 256, 256, tap_term(1, b))
    send_core(0)
    loads[8].wait()
    back = jnp.zeros((320, 256), F32)
    for a in range(3):
        for b in range(3):
            top3, top4 = (2 - a) * 32, (2 - a) * 16
            patch = jnp.concatenate(
                [dx3[b, top3 : top3 + 256, :], dx4[b, top4 : top4 + 64, :]], axis=0
            )
            back = back + nt(patch, hw[3 * a + b])
    back_s[...] = back
    for b in range(3):
        part[b * 256 : b * 256 + 256, :] = tap_term(0, b)
        part[768 + b * 256 : 1024 + b * 256, :] = tap_term(2, b)
    loads[9].wait()
    loads[10].wait()
    c3t[...] = jnp.transpose(tc3[...])
    c4t[...] = jnp.transpose(tc4[...])
    inner = back_s[32:224, :].astype(BF16)
    early[...] = nn(c3t[:, 32:224], inner)
    loads[11].wait()
    loads[12].wait()
    t3[32:224, :] = nt(inner, l3[...]).astype(BF16)

    for cp in halos:
        cp.wait_recv()
    low = jnp.where(row < 31, halo_r[0].astype(F32), 0.0)
    top = jnp.where(row > 0, halo_r[1].astype(F32), 0.0)
    zero = jnp.zeros((48, 256), F32)

    def three(val):
        i = lax.broadcasted_iota(jnp.int32, (48, 256), 0)
        last = jnp.logical_or(i == 31, i == 47)
        start = jnp.logical_or(i == 0, i == 32)
        ahead = jnp.where(last, 0.0, pltpu.roll(val, 47, 0))
        behind = jnp.where(start, 0.0, pltpu.roll(val, 1, 0))
        return [v.astype(BF16) for v in (ahead, val, behind)]

    top3 = three(top)
    low3 = three(low)
    add_top = zero
    add_low = zero
    for b in range(3):
        add_top = add_top + nt(top3[b], hw[6 + b])
        add_low = add_low + nt(low3[b], hw[b])
    back_s[0:32, :] += add_top[0:32]
    back_s[224:256, :] += add_low[0:32]
    back_s[256:272, :] += add_top[32:48]
    back_s[304:320, :] += add_low[32:48]

    for b in range(3):
        emit(b * 256, 256, part[b * 256 : b * 256 + 256, :] + nn(edge_t[1], low3[b]))
    send_core(1)
    for b in range(3):
        emit(
            1536 + b * 256, 256,
            part[768 + b * 256 : 1024 + b * 256, :] + nn(edge_t[0], top3[b]),
        )
    send_core(2)

    back3 = back_s[0:256, :]
    lat3 = back3.astype(BF16)
    rest = (back3 - lat3.astype(F32)).astype(BF16)
    cell4 = lax.broadcasted_iota(jnp.int32, (64, 256), 0)
    cell3 = lax.broadcasted_iota(jnp.int32, (64, 256), 1)
    home = (cell3 // 64) * 16 + lax.rem(cell3, 32) // 2
    pool = jnp.where(home == cell4, 1.0, 0.0).astype(BF16)
    pooled = nn(pool, lat3) + nn(pool, rest)
    lat4 = (back_s[256:320, :] + pooled).astype(BF16)
    emit(
        ROW_C3, 512,
        early[...] + nn(c3t[:, 0:32], lat3[0:32]) + nn(c3t[:, 224:256], lat3[224:256]),
    )
    send_core(3)
    emit(ROW_C4, 1024, nn(c4t[...], lat4))
    send_core(4)


    def block(at):
        return grads[at : at + 16, :] + core_r[at : at + 16, :].astype(F32)

    def pack(half, kinds):
        for xx in range(4):
            xh, xl = xx // 2, xx % 2
            for yy in range(4):
                for kind in range(kinds[0], kinds[0] + kinds[1]):
                    pair = 8 * half + (kind - 2 * yy - xl) % 8
                    r = 2 * pair + xh
                    if kind < 4:
                        val = block(144 * pair + 80 * xh + 16 * kind)
                    elif kind == 4:
                        split = block(144 * pair + 64)
                        val = jnp.concatenate([split[8 * xh : 8 * xh + 8], bias_rows], axis=0)
                    elif kind == 5:
                        val = block(ROW_C3 + 16 * r)
                    else:
                        val = block(ROW_C4 + 32 * r + 16 * (kind - 6))
                    if half:
                        by[yy, kind, xx] = val.astype(BF16)
                    else:
                        bx[xx, kind, yy] = val.astype(BF16)

    def send_first(src, at, dst, who, kinds, base):
        out = []
        for d in (2, 1, 3):
            cp = pltpu.make_async_remote_copy(
                src_ref=src.at[lax.rem(at + d, 4), pl.ds(*kinds)],
                dst_ref=dst.at[d - 1, pl.ds(*kinds)],
                send_sem=s1_ss.at[base + d - 1], recv_sem=s1_rs.at[base + d - 1],
                device_id=who[d - 1], device_id_type=MESH,
            )
            cp.start()
            out.append(cp)
        return out

    def send_second(src, at, dst, who, kinds, base):
        out = []
        for d in (2, 1, 3):
            cp = pltpu.make_async_remote_copy(
                src_ref=src.at[lax.rem(at + d, 4), pl.ds(*kinds)],
                dst_ref=dst.at[d - 1, pl.ds(*kinds)],
                send_sem=s2_ss.at[base + d - 1], recv_sem=s2_rs.at[base + d - 1],
                device_id=who[d - 1], device_id_type=MESH,
            )
            cp.start()
            out.append(cp)
        return out

    def add_first(copies, src, at, got, out, kinds):
        for cp in copies:
            cp.wait_recv()
        for k in range(kinds[0], kinds[0] + kinds[1]):
            acc = src[at, k].astype(F32)
            for d in range(3):
                acc = acc + got[d, k].astype(F32)
            for i in range(4):
                out[i, k] = acc[i].astype(BF16)

    def add_second(copies, src, at, got, base, kinds):
        for cp in copies:
            cp.wait_recv()
        lo, n = kinds
        acc = src[at, lo : lo + n].astype(F32)
        for d in range(3):
            acc = acc + got[d, lo : lo + n].astype(F32)
        dz[base + lo : base + lo + n] = acc.astype(BF16)

    for cp in core_copies[:3]:
        cp.wait_recv()
    bias_rows = block(ROW_BIAS)[0:8]
    pack(0, EARLY)
    s1xa = send_first(bx, x, r1x, x_dev, EARLY, 0)
    pack(1, EARLY)
    s1ya = send_first(by, y, r1y, y_dev, EARLY, 3)

    t3[0:32, :] = nt(lat3[0:32], l3[...]).astype(BF16)
    t3[224:256, :] = nt(lat3[224:256], l3[...]).astype(BF16)
    t4[...] = nt(lat4, l4[...]).astype(BF16)

    for cp in core_copies[3:]:
        cp.wait_recv()
    pack(0, LATE)
    s1xb = send_first(bx, x, r1x, x_dev, LATE, 6)
    pack(1, LATE)
    s1yb = send_first(by, y, r1y, y_dev, LATE, 9)
    sends = list(halos) + list(core_copies) + s1xa + s1ya + s1xb + s1yb

    add_first(s1xa, bx, x, r1x, cx, EARLY)
    s2xa = send_second(cx, y, r2x, y_dev, EARLY, 0)
    add_first(s1ya, by, y, r1y, cy, EARLY)
    s2ya = send_second(cy, x, r2y, x_dev, EARLY, 3)
    add_first(s1xb, bx, x, r1x, cx, LATE)
    s2xb = send_second(cx, y, r2x, y_dev, LATE, 6)
    add_first(s1yb, by, y, r1y, cy, LATE)
    s2yb = send_second(cy, x, r2y, x_dev, LATE, 9)
    sends += s2xa + s2ya + s2xb + s2yb

    target = 2 * y + x_lo

    def slot(zz):
        return 8 * (zz // 8) + lax.rem(zz + target, 8)

    def z_copy(at, d):
        return pltpu.make_async_remote_copy(
            src_ref=dz.at[at], dst_ref=r3.at[d], send_sem=z_ss.at[d], recv_sem=z_rs.at[d],
            device_id=z_dev(d), device_id_type=MESH,
        )

    def send_z(early):
        for d in Z_ORDER:
            zz = lax.rem(z + d, 16)

            @pl.when((lax.rem(zz + target, 8) < 5) == early)
            def _():
                z_copy(slot(zz), d).start()

    add_second(s2xa, cx, y, r2x, 0, EARLY)
    add_second(s2ya, cy, x, r2y, 8, EARLY)
    pl.semaphore_wait(far_sem, 2)
    send_z(True)
    add_second(s2xb, cx, y, r2x, 0, LATE)
    add_second(s2yb, cy, x, r2y, 8, LATE)
    send_z(False)

    acc = dz[slot(z)].astype(F32)
    for d in reversed(Z_ORDER):
        z_copy(0, d).wait_recv()
        acc = acc + r3[d].astype(F32)

    piece[...] = (acc * (1.0 / LOSS_SCALE)).astype(BF16)
    home_slot = 2 * lax.rem(z + target, 8) + core
    gath[home_slot] = piece[...]
    gathers = []
    for o in SLIDE_ORDER:
        dy, dx, dc = o // 4, (o // 2) % 2, o % 2
        xl = lax.rem(x_lo + dx, 2)
        cc = lax.rem(core + dc, 2)
        cp = pltpu.make_async_remote_copy(
            src_ref=piece, dst_ref=gath.at[home_slot], send_sem=ag_ss.at[o],
            recv_sem=ag_rs.at[o], device_id=dev(2 * x_hi + xl, lax.rem(y + dy, 4), z, cc),
            device_id_type=MESH,
        )
        cp.start()
        gathers.append(cp)
    for cp in sends:
        cp.wait_send()
    for d in Z_ORDER:
        z_copy(0, d).wait_send()
    for cp in gathers:
        cp.wait()


def finish(t3, t4, gath, o_t3, o_t4, o_head, o_bias, o_l3, o_l4):
    row = lax.axis_index("row")
    o_t3[...] = t3[...]
    o_t4[...] = t4[...]
    odd = lax.rem(row, 2)
    halves = [gath[8 + c].astype(F32) for c in range(2)]
    for c in range(2):
        lanes = slice(128 * c, 128 * c + 128)

        @pl.when(odd == 0)
        def _():
            for blk in range(4):
                o_head[16 * blk : 16 * blk + 16, lanes] = gath[2 * blk + c].astype(F32)
            o_head[64:72, lanes] = halves[c][0:8]

        @pl.when(odd == 1)
        def _():
            o_head[0:8, lanes] = halves[c][0:8]
            for blk in range(4):
                o_head[8 + 16 * blk : 24 + 16 * blk, lanes] = gath[2 * blk + c].astype(F32)

        o_l3[:, lanes] = gath[10 + c].astype(F32)
        o_l4[0:16, lanes] = gath[12 + c].astype(F32)
        o_l4[16:32, lanes] = gath[14 + c].astype(F32)
    sums = jnp.concatenate([halves[0][8:16], halves[1][8:16]], axis=1)
    lane = lax.broadcasted_iota(jnp.int32, (8, 256), 1)
    sub = lax.broadcasted_iota(jnp.int32, (8, 256), 0)
    mine = jnp.where(lane == 8 * row + sub, sums, 0.0)
    for i in range(8):
        o_bias[i] = jnp.sum(mine[i : i + 1, :])


def local(*args):
    shapes = (
        (256, 512), (64, 1024), (256, 256), (64, 256), (256, 256), (64, 256), (256, 256),
        (64, 256), (8, 32), (4, 16), (9, 256, 256), (512, 256), (1024, 256),
    )
    flat = [a.reshape(s) for a, s in zip(args, shapes)]
    vm = pltpu.VMEM
    dma = pltpu.SemaphoreType.DMA
    in_vmem = pl.BlockSpec(memory_space=vm)
    anywhere = pl.BlockSpec(memory_space=pl.ANY)
    t3, t4, gath = pl.pallas_call(
        kernel,
        out_shape=(
            vm((256, 512), BF16), vm((64, 1024), BF16), vm((16, 16, 128), BF16),
        ),
        in_specs=[anywhere] * 13,
        out_specs=(in_vmem,) * 3,
        scratch_shapes=[
            vm((16, 128), BF16),
        ] + [vm(a.shape, a.dtype) for a in flat] + [
            vm((256, 256), BF16), vm((256, 64), BF16), vm((512, 256), BF16),
            vm((1024, 64), BF16), vm((2, 256, 48), BF16),
            vm((3, 320, 256), BF16), vm((3, 96, 256), BF16),
            vm((2, 48, 256), BF16), vm((2, 48, 256), BF16),
            vm((1536, 256), F32), vm((320, 256), F32), vm((512, 256), F32),
            vm((ROWS, 128), F32), vm((ROWS, 128), BF16), vm((ROWS, 128), BF16),
            vm((4, 8, 4, 16, 128), BF16), vm((4, 8, 4, 16, 128), BF16),
            vm((3, 8, 4, 16, 128), BF16), vm((3, 8, 4, 16, 128), BF16),
            vm((4, 8, 16, 128), BF16), vm((4, 8, 16, 128), BF16),
            vm((3, 8, 16, 128), BF16), vm((3, 8, 16, 128), BF16),
            vm((16, 16, 128), BF16), vm((16, 16, 128), BF16),
            dma((13,)), dma((2,)), dma((2,)), dma((5,)), dma((5,)), dma((12,)), dma((12,)),
            dma((12,)), dma((12,)), dma((16,)), dma((16,)), dma((16,)), dma((16,)),
            pltpu.SemaphoreType.REGULAR,
        ],
        compiler_params=pltpu.CompilerParams(
            collective_id=0, has_side_effects=True, vmem_limit_bytes=56 << 20
        ),
        name="pyramid_backward",
    )(*flat)
    outs = pl.pallas_call(
        finish,
        out_shape=(
            jax.ShapeDtypeStruct((256, 512), BF16),
            jax.ShapeDtypeStruct((64, 1024), BF16),
            jax.ShapeDtypeStruct((72, 256), F32),
            jax.ShapeDtypeStruct((8,), F32),
            jax.ShapeDtypeStruct((16, 256), F32),
            jax.ShapeDtypeStruct((32, 256), F32),
        ),
        in_specs=[in_vmem] * 3,
        out_specs=(
            in_vmem, in_vmem, in_vmem, pl.BlockSpec(memory_space=pltpu.SMEM), in_vmem, in_vmem,
        ),
        name="place_outputs",
    )(*[pltpu.with_memory_space_constraint(a, vm) for a in (t3, t4, gath)])
    t3, t4, head, bias, lat3, lat4 = outs
    return (t3.reshape(1, 8, 32, 512), t4.reshape(1, 4, 16, 1024), head, bias, lat3, lat4)


def solution(mesh):
    big = P("slide", "row", None, None)
    in_specs = (big,) * 8 + (P("slide", "row", None),) * 2 + (P(),) * 3
    out_specs = (big, big, P("row", None), P("row"), P("row", None), P("row", None))
    return jax.shard_map(local, mesh=mesh, in_specs=in_specs, out_specs=out_specs, check_vma=False)
```

time: 59 us -> 47.8 us (0.81)
  local copies, waits for them, and re-layouts: 8.56 us -> 0 us
  Pallas kernels: 49.4 us -> 47 us
    unnamed x6 -> x0, local copies, waits for them, and re-layouts: 8.56 us -> none
    pallas_call x1 -> x2, Pallas kernels: 49.4 us -> 47 us  [the longest x1 46.2 us: local(): pl.pallas_call(kernel, out_shape=(vm((256, 512), BF16), vm((64, 1024), BF...]
where the time goes in v2:
time: 47.8 us; the launch traced here: 47.7 us
  Pallas kernels  47 us (98%)
  between operations  0.65 us (1%)
    pallas_call x1, Pallas kernels, local(): pl.pallas_call(kernel, out_shape=(vm((256, 512), BF16), vm((64, 1024), BF...  46.2 us

profile of v2, /device:TPU:1, one launch (start us, length us, event | category | flops | bytes accessed | tf_op | source)
XLA Modules:
  0.0 47.7 jit_solution(8984976226303426284)
XLA Ops:
  0.6 46.2 %pyramid_backward.1 = (bf16[256,512]{1,0:T(8,128)(2,1)S(1)}, bf16[64,1024]{1,0:T(8,128)(2,1)S(1)}, bf16[16,16,128]{2,1,0:T(8,128)(2,1)S(1)}) custom-call(bf16[256,512]{1,0:T(8,128)(2,1)} %bitcast.12, bf16[64,1024]{1,0:T(8,128)(2,1)} %bitcast.13, bf16[256,256]{1,0:T(8,128)(2,1)} %bitcast.14, bf16[64,256]{1,0:T(8,128)(2,1)} %bitcast.17, ...), custom_call_target="tpu_custom_call" | custom-call | tf_op jit(solution)/shard_map/pyramid_backward/pallas_call | solution.py:432
  46.9 0.8 %place_outputs.1 = (bf16[256,512]{1,0:T(8,128)(2,1)}, bf16[64,1024]{1,0:T(8,128)(2,1)}, f32[72,256]{1,0:T(8,128)}, f32[8]{0:T(128)}, f32[16,256]{1,0:T(8,128)}, /*index=5*/f32[32,256]{1,0:T(8,128)}) custom-call(bf16[256,512]{1,0:T(8,128)(2,1)S(1)} %get-tuple-element.15.t3, bf16[64,1024]{1,0:T(8,128)(2,1)S(1)} %get-tuple-element.16.t4, ...), custom_call_target="tpu_custom_call" | custom-call | tf_op jit(solution)/shard_map/place_outputs/pallas_call | solution.py:462

commit v3 on v2

v3 whole, which is shorter than its diff:
```python
import jax
import jax.numpy as jnp
from jax import lax
from jax.experimental import pallas as pl
from jax.experimental.pallas import tpu as pltpu
from jax.sharding import PartitionSpec as P

MESH = pl.DeviceIdType.MESH
F32 = jnp.float32
BF16 = jnp.bfloat16
LOSS_SCALE = 256.0

ROW_BIAS = 2304
ROW_C3 = 2320
ROW_C4 = 2832
ROWS = 3856
ROWS_EARLY, ROWS_LATE = (0, ROW_BIAS), (ROW_BIAS, ROWS - ROW_BIAS)
EARLY, LATE = (0, 4), (4, 4)
P3, G3, P4, G4, F3, F4, HW, L3, L4, WIDE = 0, 256, 512, 576, 640, 896, 960, 3264, 3776, 4800
Z_ORDER = (8, 7, 9, 6, 10, 5, 11, 4, 12, 3, 13, 2, 14, 1, 15)
SLIDE_ORDER = (11, 10, 9, 8, 7, 15, 6, 14, 5, 13, 4, 12, 3, 2, 1)


def nt(a, b):
    return lax.dot_general(a, b, (((1,), (1,)), ((), ())), preferred_element_type=F32)


def nn(a, b):
    return jnp.dot(a, b, preferred_element_type=F32)


def kernel(
    tc3_h, tc4_h, f3_h, f4_h, p3_h, p4_h, g3_h, g4_h, k3_h, k4_h, hw_h, l3_h, l4_h,
    t3, t4, gath,
    piece, wide, tc3, tc4, k3, k4,
    f3t, f4t, c3t, c4t, edge_t, dx3, dx4, halo_s, halo_r, part, back_s, early, grads,
    core_s, core_r, bx, by, r1x, r1y, cx, cy, r2x, r2y, dz, r3,
    in_sem, halo_ss, halo_rs, core_ss, core_rs, s1_ss, s1_rs, s2_ss, s2_rs,
    z_ss, z_rs, ag_ss, ag_rs, far_sem,
):
    slide = lax.axis_index("slide")
    row = lax.axis_index("row")
    core = lax.rem(slide, 2)
    x_lo = lax.rem(slide // 2, 2)
    y = slide // 4
    z = row // 2
    x_hi = lax.rem(row, 2)
    x = 2 * x_hi + x_lo

    def dev(xx, yy, zz, cc):
        return ((yy * 2 + lax.rem(xx, 2)) * 2 + cc, zz * 2 + xx // 2)

    sibling = (slide + 1 - 2 * core, row)
    above = (slide, lax.rem(row + 31, 32))
    below = (slide, lax.rem(row + 1, 32))
    x_dev = [dev(lax.rem(x + d, 4), y, z, core) for d in (1, 2, 3)]
    y_dev = [dev(x, lax.rem(y + d, 4), z, core) for d in (1, 2, 3)]

    def z_dev(d):
        return dev(x, y, lax.rem(z + d + 16, 16), core)

    def load(src, dst, i):
        pltpu.make_async_copy(src, dst, in_sem.at[i]).start()

    def load_wide(src, at, rows, i):
        load(src, wide.at[pl.ds(at, rows)], i)

    def loaded(ref, i):
        pltpu.make_async_copy(ref, ref, in_sem.at[i]).wait()

    barrier = pltpu.get_barrier_semaphore()
    partners = [above, below]
    partners += [z_dev(d) for d in (-4, 4, -3, 3, -2, 2, -1, 1)] + x_dev + y_dev + [sibling]
    load_wide(p3_h, P3, 256, 0)
    load_wide(g3_h, G3, 256, 0)
    load_wide(p4_h, P4, 64, 0)
    load_wide(g4_h, G4, 64, 0)
    load(k3_h, k3, 1)
    load(k4_h, k4, 2)
    for who in partners:
        pl.semaphore_signal(barrier, inc=1, device_id=who, device_id_type=MESH)

    loaded(wide.at[pl.ds(0, 640)], 0)
    loaded(k3, 1)
    loaded(k4, 2)
    load_wide(f3_h, F3, 256, 3)
    load_wide(f4_h, F4, 64, 3)
    load_wide(hw_h, HW, 2304, 3)
    load_wide(l3_h, L3, 512, 3)
    load_wide(l4_h, L4, 1024, 3)
    load(tc3_h, tc3, 4)
    load(tc4_h, tc4, 5)

    def delta(keep, pre, grad, height, width):
        keep_t = jnp.transpose(keep[...].astype(F32))
        cols = [jnp.broadcast_to(keep_t[:, i : i + 1], (width, 256)) for i in range(height)]
        mask = jnp.concatenate(cols, axis=0)
        cells = height * width
        live = jnp.logical_and(mask > 0.5, wide[pre : pre + cells, :].astype(F32) > 0.0)
        return jnp.where(live, wide[grad : grad + cells, :].astype(F32), 0.0)

    def put_shifted(dst, start, rows, width, val):
        col = lax.rem(lax.broadcasted_iota(jnp.int32, (rows, 256), 0), width)
        ahead = jnp.where(col == width - 1, 0.0, pltpu.roll(val, rows - 1, 0))
        behind = jnp.where(col == 0, 0.0, pltpu.roll(val, 1, 0))
        dst[0, start : start + rows, :] = ahead.astype(BF16)
        dst[1, start : start + rows, :] = val.astype(BF16)
        dst[2, start : start + rows, :] = behind.astype(BF16)

    d3 = delta(k3, P3, G3, 8, 32)
    d4 = delta(k4, P4, G4, 4, 16)
    halo_s[0, 0:32, :] = d3[0:32].astype(BF16)
    halo_s[0, 32:48, :] = d4[0:16].astype(BF16)
    halo_s[1, 0:32, :] = d3[224:256].astype(BF16)
    halo_s[1, 32:48, :] = d4[48:64].astype(BF16)

    pl.semaphore_wait(barrier, len(partners))
    for i, who in enumerate((above, below)):
        pltpu.make_async_remote_copy(
            src_ref=halo_s.at[i], dst_ref=halo_r.at[i], send_sem=halo_ss.at[0],
            recv_sem=halo_rs.at[i], device_id=who, device_id_type=MESH,
        ).start()
    for d in (-4, 4):
        pl.semaphore_signal(far_sem, inc=1, device_id=z_dev(d), device_id_type=MESH)

    put_shifted(dx3, 32, 256, 32, d3)
    put_shifted(dx4, 16, 64, 16, d4)
    for b in range(3):
        dx3[b, 0:32, :] = jnp.zeros((32, 256), BF16)
        dx3[b, 288:320, :] = jnp.zeros((32, 256), BF16)
        dx4[b, 0:16, :] = jnp.zeros((16, 256), BF16)
        dx4[b, 80:96, :] = jnp.zeros((16, 256), BF16)

    first = core == 0

    def emit(start, rows, val):
        lo, hi = val[:, :128], val[:, 128:]
        at = pl.ds(start, rows)
        grads[at, :] = jnp.where(first, lo, hi)
        core_s[at, :] = jnp.where(first, hi, lo).astype(BF16)

    def core_copy(start, rows, i):
        at = pl.ds(start, rows)
        return pltpu.make_async_remote_copy(
            src_ref=core_s.at[at], dst_ref=core_r.at[at], send_sem=core_ss.at[0],
            recv_sem=core_rs.at[i], device_id=sibling, device_id_type=MESH,
        )

    ones = jnp.ones((16, 256), BF16)
    bias = nn(ones, dx3[1, 32:288, :]) + nn(ones[:, :64], dx4[1, 16:80, :])
    emit(ROW_BIAS, 16, bias)
    loaded(wide.at[pl.ds(F3, WIDE - F3)], 3)
    f3t[...] = jnp.transpose(wide[F3 : F3 + 256, :])
    f4t[...] = jnp.transpose(wide[F4 : F4 + 64, :])
    for i, (at3, at4) in enumerate(((F3, F4), (F3 + 224, F4 + 48))):
        edge = jnp.concatenate([wide[at3 : at3 + 32, :], wide[at4 : at4 + 16, :]], axis=0)
        edge_t[i] = jnp.transpose(edge)

    def tap_term(a, b):
        top3, top4 = (2 - a) * 32, (2 - a) * 16
        val = nn(f3t[...], dx3[b, top3 : top3 + 256, :])
        return val + nn(f4t[...], dx4[b, top4 : top4 + 64, :])

    for b in range(3):
        emit((3 + b) * 256, 256, tap_term(1, b))
    core_copy(768, 768, 0).start()
    back = jnp.zeros((320, 256), F32)
    for a in range(3):
        for b in range(3):
            top3, top4 = (2 - a) * 32, (2 - a) * 16
            patch = jnp.concatenate(
                [dx3[b, top3 : top3 + 256, :], dx4[b, top4 : top4 + 64, :]], axis=0
            )
            at = HW + 256 * (3 * a + b)
            back = back + nt(patch, wide[at : at + 256, :])
    back_s[...] = back
    for b in range(3):
        part[b * 256 : b * 256 + 256, :] = tap_term(0, b)
        part[768 + b * 256 : 1024 + b * 256, :] = tap_term(2, b)
    loaded(tc3, 4)
    loaded(tc4, 5)
    c3t[...] = jnp.transpose(tc3[...])
    c4t[...] = jnp.transpose(tc4[...])
    inner = back_s[32:224, :].astype(BF16)
    early[...] = nn(c3t[:, 32:224], inner)
    l3, l4 = wide[L3 : L3 + 512, :], wide[L4 : L4 + 1024, :]
    t3[32:224, :] = nt(inner, l3).astype(BF16)

    def three(val):
        i = lax.broadcasted_iota(jnp.int32, (48, 256), 0)
        last = jnp.logical_or(i == 31, i == 47)
        start = jnp.logical_or(i == 0, i == 32)
        ahead = jnp.where(last, 0.0, pltpu.roll(val, 47, 0))
        behind = jnp.where(start, 0.0, pltpu.roll(val, 1, 0))
        return [v.astype(BF16) for v in (ahead, val, behind)]

    def edge_side(side):
        pltpu.make_async_remote_copy(
            src_ref=halo_s.at[side], dst_ref=halo_r.at[side], send_sem=halo_ss.at[0],
            recv_sem=halo_rs.at[side], device_id=above, device_id_type=MESH,
        ).wait_recv()
        valid = jnp.where(side == 0, row, 31 - row) < 31
        shifted = three(jnp.where(valid, halo_r[side].astype(F32), 0.0))
        start = pl.multiple_of(side * 1536, 256)
        half = pl.multiple_of(side * 768, 256)
        for b in range(3):
            val = part[pl.ds(half + b * 256, 256), :] + nn(edge_t[1 - side], shifted[b])
            emit(start + b * 256, 256, val)
        core_copy(start, 768, 0).start()
        add = jnp.zeros((48, 256), F32)
        for b in range(3):
            at = pl.multiple_of(HW + 1536 * side + 256 * b, 64)
            add = add + nt(shifted[b], wide[pl.ds(at, 256), :])
        at3 = pl.ds(pl.multiple_of(224 * (1 - side), 32), 32)
        at4 = pl.ds(pl.multiple_of(256 + 48 * (1 - side), 16), 16)
        back_s[at3, :] += add[0:32]
        back_s[at4, :] += add[32:48]

    edge_side(x_hi)
    edge_side(1 - x_hi)

    back3 = back_s[0:256, :]
    lat3 = back3.astype(BF16)
    rest = (back3 - lat3.astype(F32)).astype(BF16)
    cell4 = lax.broadcasted_iota(jnp.int32, (64, 256), 0)
    cell3 = lax.broadcasted_iota(jnp.int32, (64, 256), 1)
    home = (cell3 // 64) * 16 + lax.rem(cell3, 32) // 2
    pool = jnp.where(home == cell4, 1.0, 0.0).astype(BF16)
    pooled = nn(pool, lat3) + nn(pool, rest)
    lat4 = (back_s[256:320, :] + pooled).astype(BF16)
    emit(
        ROW_C3, 512,
        early[...] + nn(c3t[:, 0:32], lat3[0:32]) + nn(c3t[:, 224:256], lat3[224:256]),
    )
    core_copy(ROW_BIAS, 528, 1).start()
    emit(ROW_C4, 1024, nn(c4t[...], lat4))
    core_copy(ROW_C4, 1024, 1).start()


    def block(at):
        return grads[at : at + 16, :] + core_r[at : at + 16, :].astype(F32)

    def pack(half, kinds, bias_rows=None):
        for xx in range(4):
            xh, xl = xx // 2, xx % 2
            for yy in range(4):
                for kind in range(kinds[0], kinds[0] + kinds[1]):
                    pair = 8 * half + (kind - 2 * yy - xl) % 8
                    r = 2 * pair + xh
                    if kind < 4:
                        val = block(144 * pair + 80 * xh + 16 * kind)
                    elif kind == 4:
                        split = block(144 * pair + 64)
                        val = jnp.concatenate([split[8 * xh : 8 * xh + 8], bias_rows], axis=0)
                    elif kind == 5:
                        val = block(ROW_C3 + 16 * r)
                    else:
                        val = block(ROW_C4 + 32 * r + 16 * (kind - 6))
                    if half:
                        by[yy, kind, xx] = val.astype(BF16)
                    else:
                        bx[xx, kind, yy] = val.astype(BF16)

    def first_copy(src, at, dst, who, kinds, axis, late):
        blocks = pl.ds(*kinds)
        return pltpu.make_async_remote_copy(
            src_ref=src.at[at, blocks], dst_ref=dst.at[who, blocks], send_sem=s1_ss.at[axis],
            recv_sem=s1_rs.at[2 * axis + late],
            device_id=(x_dev, y_dev)[axis][who], device_id_type=MESH,
        )

    def send_first(src, at, dst, kinds, axis, late):
        for d in (2, 1, 3):
            first_copy(src, lax.rem(at + d, 4), dst, d - 1, kinds, axis, late).start()

    def second_copy(src, at, dst, who, kinds, axis, late):
        blocks = pl.ds(*kinds)
        return pltpu.make_async_remote_copy(
            src_ref=src.at[at, blocks], dst_ref=dst.at[who, blocks], send_sem=s2_ss.at[axis],
            recv_sem=s2_rs.at[2 * axis + late],
            device_id=(x_dev, y_dev)[axis][who], device_id_type=MESH,
        )

    def send_second(src, at, dst, kinds, axis, late):
        for d in (2, 1, 3):
            second_copy(src, lax.rem(at + d, 4), dst, d - 1, kinds, axis, late).start()

    def arrived(ref, sem):
        pltpu.make_async_copy(ref, ref, sem).wait()

    def add_first(src, at, got, out, kinds, axis, late):
        arrived(got.at[:, pl.ds(*kinds)], s1_rs.at[2 * axis + late])
        for k in range(kinds[0], kinds[0] + kinds[1]):
            acc = src[at, k].astype(F32)
            for d in range(3):
                acc = acc + got[d, k].astype(F32)
            for i in range(4):
                out[i, k] = acc[i].astype(BF16)

    def add_second(src, at, got, base, kinds, axis, late):
        arrived(got.at[:, pl.ds(*kinds)], s2_rs.at[2 * axis + late])
        lo, n = kinds
        acc = src[at, lo : lo + n].astype(F32)
        for d in range(3):
            acc = acc + got[d, lo : lo + n].astype(F32)
        dz[base + lo : base + lo + n] = acc.astype(BF16)

    arrived(core_r.at[pl.ds(*ROWS_EARLY)], core_rs.at[0])
    pack(0, EARLY)
    send_first(bx, x, r1x, EARLY, 0, 0)
    pack(1, EARLY)
    send_first(by, y, r1y, EARLY, 1, 0)

    t3[0:32, :] = nt(lat3[0:32], l3).astype(BF16)
    t3[224:256, :] = nt(lat3[224:256], l3).astype(BF16)
    t4[...] = nt(lat4, l4).astype(BF16)

    arrived(core_r.at[pl.ds(*ROWS_LATE)], core_rs.at[1])
    bias_rows = block(ROW_BIAS)[0:8]
    pack(0, LATE, bias_rows)
    send_first(bx, x, r1x, LATE, 0, 1)
    pack(1, LATE, bias_rows)
    send_first(by, y, r1y, LATE, 1, 1)

    add_first(bx, x, r1x, cx, EARLY, 0, 0)
    send_second(cx, y, r2x, EARLY, 1, 0)
    add_first(by, y, r1y, cy, EARLY, 1, 0)
    send_second(cy, x, r2y, EARLY, 0, 0)
    add_first(bx, x, r1x, cx, LATE, 0, 1)
    send_second(cx, y, r2x, LATE, 1, 1)
    add_first(by, y, r1y, cy, LATE, 1, 1)
    send_second(cy, x, r2y, LATE, 0, 1)

    target = 2 * y + x_lo

    def slot(zz):
        return 8 * (zz // 8) + lax.rem(zz + target, 8)

    def z_copy(at, d):
        return pltpu.make_async_remote_copy(
            src_ref=dz.at[at], dst_ref=r3.at[d], send_sem=z_ss.at[0], recv_sem=z_rs.at[0],
            device_id=z_dev(d), device_id_type=MESH,
        )

    def send_z(early):
        for d in Z_ORDER:
            zz = lax.rem(z + d, 16)

            @pl.when((lax.rem(zz + target, 8) < 4) == early)
            def _():
                z_copy(slot(zz), d).start()

    add_second(cx, y, r2x, 0, EARLY, 1, 0)
    add_second(cy, x, r2y, 8, EARLY, 0, 0)
    pl.semaphore_wait(far_sem, 2)
    send_z(True)
    add_second(cx, y, r2x, 0, LATE, 1, 1)
    add_second(cy, x, r2y, 8, LATE, 0, 1)
    send_z(False)

    arrived(r3.at[pl.ds(1, 15)], z_rs.at[0])
    acc = dz[slot(z)].astype(F32)
    for d in range(1, 16):
        acc = acc + r3[d].astype(F32)

    piece[...] = (acc * (1.0 / LOSS_SCALE)).astype(BF16)
    home_slot = 2 * lax.rem(z + target, 8) + core
    gath[home_slot] = piece[...]
    for o in SLIDE_ORDER:
        dy, dx, dc = o // 4, (o // 2) % 2, o % 2
        xl = lax.rem(x_lo + dx, 2)
        cc = lax.rem(core + dc, 2)
        pltpu.make_async_remote_copy(
            src_ref=piece, dst_ref=gath.at[home_slot], send_sem=ag_ss.at[0],
            recv_sem=ag_rs.at[0], device_id=dev(2 * x_hi + xl, lax.rem(y + dy, 4), z, cc),
            device_id_type=MESH,
        ).start()

    arrived(halo_s, halo_ss.at[0])
    arrived(core_s, core_ss.at[0])
    for axis in range(2):
        arrived(bx.at[pl.ds(0, 3)], s1_ss.at[axis])
        arrived(cx.at[pl.ds(0, 3)], s2_ss.at[axis])
    arrived(dz.at[pl.ds(0, 15)], z_ss.at[0])
    arrived(gath.at[pl.ds(0, 15)], ag_ss.at[0])
    arrived(gath.at[pl.ds(0, 15)], ag_rs.at[0])


def finish(t3, t4, gath, o_t3, o_t4, o_head, o_bias, o_l3, o_l4):
    row = lax.axis_index("row")
    o_t3[...] = t3[...]
    o_t4[...] = t4[...]
    odd = lax.rem(row, 2)
    halves = [gath[8 + c].astype(F32) for c in range(2)]
    for c in range(2):
        lanes = slice(128 * c, 128 * c + 128)

        @pl.when(odd == 0)
        def _():
            for blk in range(4):
                o_head[16 * blk : 16 * blk + 16, lanes] = gath[2 * blk + c].astype(F32)
            o_head[64:72, lanes] = halves[c][0:8]

        @pl.when(odd == 1)
        def _():
            o_head[0:8, lanes] = halves[c][0:8]
            for blk in range(4):
                o_head[8 + 16 * blk : 24 + 16 * blk, lanes] = gath[2 * blk + c].astype(F32)

        o_l3[:, lanes] = gath[10 + c].astype(F32)
        o_l4[0:16, lanes] = gath[12 + c].astype(F32)
        o_l4[16:32, lanes] = gath[14 + c].astype(F32)
    sums = jnp.concatenate([halves[0][8:16], halves[1][8:16]], axis=1)
    lane = lax.broadcasted_iota(jnp.int32, (8, 256), 1)
    sub = lax.broadcasted_iota(jnp.int32, (8, 256), 0)
    mine = jnp.where(lane == 8 * row + sub, sums, 0.0)
    for i in range(8):
        o_bias[i] = jnp.sum(mine[i : i + 1, :])


def local(*args):
    shapes = (
        (256, 512), (64, 1024), (256, 256), (64, 256), (256, 256), (64, 256), (256, 256),
        (64, 256), (8, 32), (4, 16), (2304, 256), (512, 256), (1024, 256),
    )
    flat = [a.reshape(s) for a, s in zip(args, shapes)]
    vm = pltpu.VMEM
    dma = pltpu.SemaphoreType.DMA
    in_vmem = pl.BlockSpec(memory_space=vm)
    anywhere = pl.BlockSpec(memory_space=pl.ANY)
    t3, t4, gath = pl.pallas_call(
        kernel,
        out_shape=(
            vm((256, 512), BF16), vm((64, 1024), BF16), vm((16, 16, 128), BF16),
        ),
        in_specs=[anywhere] * 13,
        out_specs=(in_vmem,) * 3,
        scratch_shapes=[
            vm((16, 128), BF16), vm((WIDE, 256), BF16), vm((256, 512), BF16),
            vm((64, 1024), BF16), vm((8, 32), jnp.int32), vm((4, 16), jnp.int32),
            vm((256, 256), BF16), vm((256, 64), BF16), vm((512, 256), BF16),
            vm((1024, 64), BF16), vm((2, 256, 48), BF16),
            vm((3, 320, 256), BF16), vm((3, 96, 256), BF16),
            vm((2, 48, 256), BF16), vm((2, 48, 256), BF16),
            vm((1536, 256), F32), vm((320, 256), F32), vm((512, 256), F32),
            vm((ROWS, 128), F32), vm((ROWS, 128), BF16), vm((ROWS, 128), BF16),
            vm((4, 8, 4, 16, 128), BF16), vm((4, 8, 4, 16, 128), BF16),
            vm((3, 8, 4, 16, 128), BF16), vm((3, 8, 4, 16, 128), BF16),
            vm((4, 8, 16, 128), BF16), vm((4, 8, 16, 128), BF16),
            vm((3, 8, 16, 128), BF16), vm((3, 8, 16, 128), BF16),
            vm((16, 16, 128), BF16), vm((16, 16, 128), BF16),
            dma((6,)), dma((1,)), dma((2,)), dma((1,)), dma((2,)), dma((2,)), dma((4,)),
            dma((2,)), dma((4,)), dma((1,)), dma((1,)), dma((1,)), dma((1,)),
            pltpu.SemaphoreType.REGULAR,
        ],
        compiler_params=pltpu.CompilerParams(
            collective_id=0, has_side_effects=True, vmem_limit_bytes=56 << 20
        ),
        name="pyramid_backward",
    )(*flat)
    outs = pl.pallas_call(
        finish,
        out_shape=(
            jax.ShapeDtypeStruct((256, 512), BF16),
            jax.ShapeDtypeStruct((64, 1024), BF16),
            jax.ShapeDtypeStruct((72, 256), F32),
            jax.ShapeDtypeStruct((8,), F32),
            jax.ShapeDtypeStruct((16, 256), F32),
            jax.ShapeDtypeStruct((32, 256), F32),
        ),
        in_specs=[in_vmem] * 3,
        out_specs=(
            in_vmem, in_vmem, in_vmem, pl.BlockSpec(memory_space=pltpu.SMEM), in_vmem, in_vmem,
        ),
        name="place_outputs",
    )(*[pltpu.with_memory_space_constraint(a, vm) for a in (t3, t4, gath)])
    t3, t4, head, bias, lat3, lat4 = outs
    return (t3.reshape(1, 8, 32, 512), t4.reshape(1, 4, 16, 1024), head, bias, lat3, lat4)


def solution(mesh):
    big = P("slide", "row", None, None)
    in_specs = (big,) * 8 + (P("slide", "row", None),) * 2 + (P(),) * 3
    out_specs = (big, big, P("row", None), P("row"), P("row", None), P("row", None))
    return jax.shard_map(local, mesh=mesh, in_specs=in_specs, out_specs=out_specs, check_vma=False)
```

time: 47.8 us -> 46.7 us (0.977)
  Pallas kernels: 47 us -> 45.9 us
    pallas_call x1, Pallas kernels: 46.2 us -> 45.1 us  [local(): pl.pallas_call(kernel, out_shape=(vm((256, 512), BF16), vm((64, 1024), BF...]
where the time goes in v3:
time: 46.7 us; the launch traced here: 46.6 us
  Pallas kernels  45.9 us (98%)
  between operations  0.65 us (1%)
    pallas_call x1, Pallas kernels, local(): pl.pallas_call(kernel, out_shape=(vm((256, 512), BF16), vm((64, 1024), BF...  45.1 us

profile of v3, /device:TPU:1, one launch (start us, length us, event | category | flops | bytes accessed | tf_op | source)
XLA Modules:
  0.0 46.6 jit_solution(16678357792705316807)
XLA Ops:
  0.6 45.1 %pyramid_backward.1 = (bf16[256,512]{1,0:T(8,128)(2,1)S(1)}, bf16[64,1024]{1,0:T(8,128)(2,1)S(1)}, bf16[16,16,128]{2,1,0:T(8,128)(2,1)S(1)}) custom-call(bf16[256,512]{1,0:T(8,128)(2,1)} %bitcast.14, bf16[64,1024]{1,0:T(8,128)(2,1)} %bitcast.15, bf16[256,256]{1,0:T(8,128)(2,1)} %bitcast.16, bf16[64,256]{1,0:T(8,128)(2,1)} %bitcast.19, ...), custom_call_target="tpu_custom_call" | custom-call | tf_op jit(solution)/shard_map/pyramid_backward/pallas_call | solution.py:431
  45.7 0.8 %place_outputs.1 = (bf16[256,512]{1,0:T(8,128)(2,1)}, bf16[64,1024]{1,0:T(8,128)(2,1)}, f32[72,256]{1,0:T(8,128)}, f32[8]{0:T(128)}, f32[16,256]{1,0:T(8,128)}, /*index=5*/f32[32,256]{1,0:T(8,128)}) custom-call(bf16[256,512]{1,0:T(8,128)(2,1)S(1)} %get-tuple-element.15.t3, bf16[64,1024]{1,0:T(8,128)(2,1)S(1)} %get-tuple-element.16.t4, ...), custom_call_target="tpu_custom_call" | custom-call | tf_op jit(solution)/shard_map/place_outputs/pallas_call | solution.py:461

commit v4 on v3

--- a/solution.py
+++ b/solution.py
@@ -14,10 +14,11 @@
 ROW_C3 = 2320
 ROW_C4 = 2832
 ROWS = 3856
-ROWS_EARLY, ROWS_LATE = (0, ROW_BIAS), (ROW_BIAS, ROWS - ROW_BIAS)
-EARLY, LATE = (0, 4), (4, 4)
+AHEAD, NEXT, REST = (0, 2), (2, 2), (4, 4)
+C3_AHEAD, C4_AHEAD = 128, 256
+ROWS_AHEAD = 768 + 16 + C3_AHEAD + C4_AHEAD
 P3, G3, P4, G4, F3, F4, HW, L3, L4, WIDE = 0, 256, 512, 576, 640, 896, 960, 3264, 3776, 4800
-Z_ORDER = (8, 7, 9, 6, 10, 5, 11, 4, 12, 3, 13, 2, 14, 1, 15)
+PLANES_REST = (15, 14, 13, 12, 11, 10, 9, 8)
 SLIDE_ORDER = (11, 10, 9, 8, 7, 15, 6, 14, 5, 13, 4, 12, 3, 2, 1)
 
 
@@ -163,7 +164,7 @@
 
     for b in range(3):
         emit((3 + b) * 256, 256, tap_term(1, b))
-    core_copy(768, 768, 0).start()
+    core_copy(768, 768, 1).start()
     back = jnp.zeros((320, 256), F32)
     for a in range(3):
         for b in range(3):
@@ -186,7 +187,13 @@
     l3, l4 = wide[L3 : L3 + 512, :], wide[L4 : L4 + 1024, :]
     t3[32:224, :] = nt(inner, l3).astype(BF16)
 
-    def three(val):
+    def edge_side(side):
+        pltpu.make_async_remote_copy(
+            src_ref=halo_s.at[side], dst_ref=halo_r.at[side], send_sem=halo_ss.at[0],
+            recv_sem=halo_rs.at[side], device_id=above, device_id_type=MESH,
+        ).wait_recv()
+        valid = row > 0 if side else row < 31
+        val = jnp.where(valid, halo_r[side].astype(F32), 0.0)
         i = lax.broadcasted_iota(jnp.int32, (48, 256), 0)
         last = jnp.logical_or(i == 31, i == 47)
         start = jnp.logical_or(i == 0, i == 32)
@@ -194,30 +201,27 @@
         behind = jnp.where(start, 0.0, pltpu.roll(val, 1, 0))
         return [v.astype(BF16) for v in (ahead, val, behind)]
 
-    def edge_side(side):
-        pltpu.make_async_remote_copy(
-            src_ref=halo_s.at[side], dst_ref=halo_r.at[side], send_sem=halo_ss.at[0],
-            recv_sem=halo_rs.at[side], device_id=above, device_id_type=MESH,
-        ).wait_recv()
-        valid = jnp.where(side == 0, row, 31 - row) < 31
-        shifted = three(jnp.where(valid, halo_r[side].astype(F32), 0.0))
-        start = pl.multiple_of(side * 1536, 256)
-        half = pl.multiple_of(side * 768, 256)
-        for b in range(3):
-            val = part[pl.ds(half + b * 256, 256), :] + nn(edge_t[1 - side], shifted[b])
-            emit(start + b * 256, 256, val)
-        core_copy(start, 768, 0).start()
+    def edge_back(side, shifted):
         add = jnp.zeros((48, 256), F32)
         for b in range(3):
-            at = pl.multiple_of(HW + 1536 * side + 256 * b, 64)
-            add = add + nt(shifted[b], wide[pl.ds(at, 256), :])
-        at3 = pl.ds(pl.multiple_of(224 * (1 - side), 32), 32)
-        at4 = pl.ds(pl.multiple_of(256 + 48 * (1 - side), 16), 16)
-        back_s[at3, :] += add[0:32]
-        back_s[at4, :] += add[32:48]
-
-    edge_side(x_hi)
-    edge_side(1 - x_hi)
+            at = HW + 1536 * side + 256 * b
+            add = add + nt(shifted[b], wide[at : at + 256, :])
+        at3, at4 = 224 * (1 - side), 256 + 48 * (1 - side)
+        back_s[at3 : at3 + 32, :] += add[0:32]
+        back_s[at4 : at4 + 16, :] += add[32:48]
+
+    def edge_head(side, shifted):
+        for b in range(3):
+            at = 768 * side + 256 * b
+            val = part[at : at + 256, :] + nn(edge_t[1 - side], shifted[b])
+            emit(1536 * side + 256 * b, 256, val)
+
+    low = edge_side(0)
+    edge_head(0, low)
+    core_copy(0, 768, 0).start()
+    edge_back(0, low)
+    top = edge_side(1)
+    edge_back(1, top)
 
     back3 = back_s[0:256, :]
     lat3 = back3.astype(BF16)
@@ -228,150 +232,159 @@
     pool = jnp.where(home == cell4, 1.0, 0.0).astype(BF16)
     pooled = nn(pool, lat3) + nn(pool, rest)
     lat4 = (back_s[256:320, :] + pooled).astype(BF16)
-    emit(
-        ROW_C3, 512,
-        early[...] + nn(c3t[:, 0:32], lat3[0:32]) + nn(c3t[:, 224:256], lat3[224:256]),
-    )
-    core_copy(ROW_BIAS, 528, 1).start()
-    emit(ROW_C4, 1024, nn(c4t[...], lat4))
-    core_copy(ROW_C4, 1024, 1).start()
-
+
+    def emit_c3(lo, hi):
+        val = early[lo:hi, :] + nn(c3t[lo:hi, 0:32], lat3[0:32])
+        val = val + nn(c3t[lo:hi, 224:256], lat3[224:256])
+        emit(ROW_C3 + lo, hi - lo, val)
+
+    def emit_c4(lo, hi):
+        emit(ROW_C4 + lo, hi - lo, nn(c4t[lo:hi, :], lat4))
+
+    emit_c3(0, C3_AHEAD)
+    core_copy(ROW_BIAS, 16 + C3_AHEAD, 0).start()
+    emit_c4(0, C4_AHEAD)
+    core_copy(ROW_C4, C4_AHEAD, 0).start()
+    edge_head(1, top)
+    core_copy(1536, 768, 1).start()
+    emit_c3(C3_AHEAD, 512)
+    core_copy(ROW_C3 + C3_AHEAD, 512 - C3_AHEAD, 1).start()
+    emit_c4(C4_AHEAD, 1024)
+    core_copy(ROW_C4 + C4_AHEAD, 1024 - C4_AHEAD, 1).start()
 
     def block(at):
         return grads[at : at + 16, :] + core_r[at : at + 16, :].astype(F32)
 
-    def pack(half, kinds, bias_rows=None):
+    def pack(half, places):
         for xx in range(4):
             xh, xl = xx // 2, xx % 2
             for yy in range(4):
-                for kind in range(kinds[0], kinds[0] + kinds[1]):
-                    pair = 8 * half + (kind - 2 * yy - xl) % 8
-                    r = 2 * pair + xh
+                kind = 2 * yy + xl
+                for place in range(places[0], places[0] + places[1]):
+                    plane = 2 * place + half
+                    r = 2 * plane + xh
                     if kind < 4:
-                        val = block(144 * pair + 80 * xh + 16 * kind)
+                        val = block(144 * plane + 80 * xh + 16 * kind)
                     elif kind == 4:
-                        split = block(144 * pair + 64)
+                        split = block(144 * plane + 64)
                         val = jnp.concatenate([split[8 * xh : 8 * xh + 8], bias_rows], axis=0)
                     elif kind == 5:
                         val = block(ROW_C3 + 16 * r)
                     else:
                         val = block(ROW_C4 + 32 * r + 16 * (kind - 6))
                     if half:
-                        by[yy, kind, xx] = val.astype(BF16)
+                        by[yy, place, xx] = val.astype(BF16)
                     else:
-                        bx[xx, kind, yy] = val.astype(BF16)
-
-    def first_copy(src, at, dst, who, kinds, axis, late):
-        blocks = pl.ds(*kinds)
-        return pltpu.make_async_remote_copy(
-            src_ref=src.at[at, blocks], dst_ref=dst.at[who, blocks], send_sem=s1_ss.at[axis],
-            recv_sem=s1_rs.at[2 * axis + late],
-            device_id=(x_dev, y_dev)[axis][who], device_id_type=MESH,
-        )
-
-    def send_first(src, at, dst, kinds, axis, late):
-        for d in (2, 1, 3):
-            first_copy(src, lax.rem(at + d, 4), dst, d - 1, kinds, axis, late).start()
-
-    def second_copy(src, at, dst, who, kinds, axis, late):
-        blocks = pl.ds(*kinds)
-        return pltpu.make_async_remote_copy(
-            src_ref=src.at[at, blocks], dst_ref=dst.at[who, blocks], send_sem=s2_ss.at[axis],
-            recv_sem=s2_rs.at[2 * axis + late],
-            device_id=(x_dev, y_dev)[axis][who], device_id_type=MESH,
-        )
-
-    def send_second(src, at, dst, kinds, axis, late):
-        for d in (2, 1, 3):
-            second_copy(src, lax.rem(at + d, 4), dst, d - 1, kinds, axis, late).start()
+                        bx[xx, place, yy] = val.astype(BF16)
 
     def arrived(ref, sem):
         pltpu.make_async_copy(ref, ref, sem).wait()
 
-    def add_first(src, at, got, out, kinds, axis, late):
-        arrived(got.at[:, pl.ds(*kinds)], s1_rs.at[2 * axis + late])
-        for k in range(kinds[0], kinds[0] + kinds[1]):
+    def send_first(src, at, dst, places, axis, group):
+        blocks = pl.ds(*places)
+        for d in (2, 1, 3):
+            pltpu.make_async_remote_copy(
+                src_ref=src.at[lax.rem(at + d, 4), blocks], dst_ref=dst.at[d - 1, blocks],
+                send_sem=s1_ss.at[axis], recv_sem=s1_rs.at[3 * axis + group],
+                device_id=(x_dev, y_dev)[axis][d - 1], device_id_type=MESH,
+            ).start()
+
+    def send_second(src, at, dst, places, axis, group):
+        blocks = pl.ds(*places)
+        for d in (2, 1, 3):
+            pltpu.make_async_remote_copy(
+                src_ref=src.at[lax.rem(at + d, 4), blocks], dst_ref=dst.at[d - 1, blocks],
+                send_sem=s2_ss.at[axis], recv_sem=s2_rs.at[3 * axis + group],
+                device_id=(x_dev, y_dev)[axis][d - 1], device_id_type=MESH,
+            ).start()
+
+    def add_first(src, at, got, out, places, axis, group):
+        arrived(got.at[:, pl.ds(*places)], s1_rs.at[3 * axis + group])
+        for k in range(places[0], places[0] + places[1]):
             acc = src[at, k].astype(F32)
             for d in range(3):
                 acc = acc + got[d, k].astype(F32)
             for i in range(4):
                 out[i, k] = acc[i].astype(BF16)
 
-    def add_second(src, at, got, base, kinds, axis, late):
-        arrived(got.at[:, pl.ds(*kinds)], s2_rs.at[2 * axis + late])
-        lo, n = kinds
+    def add_second(src, at, got, base, places, axis, group):
+        arrived(got.at[:, pl.ds(*places)], s2_rs.at[3 * axis + group])
+        lo, n = places
         acc = src[at, lo : lo + n].astype(F32)
         for d in range(3):
             acc = acc + got[d, lo : lo + n].astype(F32)
         dz[base + lo : base + lo + n] = acc.astype(BF16)
 
-    arrived(core_r.at[pl.ds(*ROWS_EARLY)], core_rs.at[0])
-    pack(0, EARLY)
-    send_first(bx, x, r1x, EARLY, 0, 0)
-    pack(1, EARLY)
-    send_first(by, y, r1y, EARLY, 1, 0)
-
+    arrived(core_r.at[pl.ds(0, ROWS_AHEAD)], core_rs.at[0])
+    bias_rows = block(ROW_BIAS)[0:8]
+    pack(0, AHEAD)
+    send_first(bx, x, r1x, AHEAD, 0, 0)
+    pack(1, AHEAD)
+    send_first(by, y, r1y, AHEAD, 1, 0)
+
+    arrived(core_r.at[pl.ds(0, ROWS - ROWS_AHEAD)], core_rs.at[1])
+    for places in (NEXT, REST):
+        pack(0, places)
+        pack(1, places)
     t3[0:32, :] = nt(lat3[0:32], l3).astype(BF16)
     t3[224:256, :] = nt(lat3[224:256], l3).astype(BF16)
     t4[...] = nt(lat4, l4).astype(BF16)
 
-    arrived(core_r.at[pl.ds(*ROWS_LATE)], core_rs.at[1])
-    bias_rows = block(ROW_BIAS)[0:8]
-    pack(0, LATE, bias_rows)
-    send_first(bx, x, r1x, LATE, 0, 1)
-    pack(1, LATE, bias_rows)
-    send_first(by, y, r1y, LATE, 1, 1)
-
-    add_first(bx, x, r1x, cx, EARLY, 0, 0)
-    send_second(cx, y, r2x, EARLY, 1, 0)
-    add_first(by, y, r1y, cy, EARLY, 1, 0)
-    send_second(cy, x, r2y, EARLY, 0, 0)
-    add_first(bx, x, r1x, cx, LATE, 0, 1)
-    send_second(cx, y, r2x, LATE, 1, 1)
-    add_first(by, y, r1y, cy, LATE, 1, 1)
-    send_second(cy, x, r2y, LATE, 0, 1)
-
-    target = 2 * y + x_lo
-
-    def slot(zz):
-        return 8 * (zz // 8) + lax.rem(zz + target, 8)
-
-    def z_copy(at, d):
-        return pltpu.make_async_remote_copy(
-            src_ref=dz.at[at], dst_ref=r3.at[d], send_sem=z_ss.at[0], recv_sem=z_rs.at[0],
-            device_id=z_dev(d), device_id_type=MESH,
-        )
-
-    def send_z(early):
-        for d in Z_ORDER:
-            zz = lax.rem(z + d, 16)
-
-            @pl.when((lax.rem(zz + target, 8) < 4) == early)
-            def _():
-                z_copy(slot(zz), d).start()
-
-    add_second(cx, y, r2x, 0, EARLY, 1, 0)
-    add_second(cy, x, r2y, 8, EARLY, 0, 0)
+    add_first(bx, x, r1x, cx, AHEAD, 0, 0)
+    send_second(cx, y, r2x, AHEAD, 1, 0)
+    add_first(by, y, r1y, cy, AHEAD, 1, 0)
+    send_second(cy, x, r2y, AHEAD, 0, 0)
+    send_first(bx, x, r1x, NEXT, 0, 1)
+    send_first(by, y, r1y, NEXT, 1, 1)
+    send_first(bx, x, r1x, REST, 0, 2)
+    send_first(by, y, r1y, REST, 1, 2)
+
+    def send_z(plane):
+        d = lax.rem(plane - z + 16, 16)
+
+        @pl.when(d != 0)
+        def _():
+            pltpu.make_async_remote_copy(
+                src_ref=dz.at[8 * (plane % 2) + plane // 2], dst_ref=r3.at[d],
+                send_sem=z_ss.at[0], recv_sem=z_rs.at[0], device_id=dev(x, y, plane, core),
+                device_id_type=MESH,
+            ).start()
+
+    add_second(cx, y, r2x, 0, AHEAD, 1, 0)
+    add_second(cy, x, r2y, 8, AHEAD, 0, 0)
     pl.semaphore_wait(far_sem, 2)
-    send_z(True)
-    add_second(cx, y, r2x, 0, LATE, 1, 1)
-    add_second(cy, x, r2y, 8, LATE, 0, 1)
-    send_z(False)
+    for plane in range(4):
+        send_z(plane)
+    add_first(bx, x, r1x, cx, NEXT, 0, 1)
+    send_second(cx, y, r2x, NEXT, 1, 1)
+    add_first(by, y, r1y, cy, NEXT, 1, 1)
+    send_second(cy, x, r2y, NEXT, 0, 1)
+    add_first(bx, x, r1x, cx, REST, 0, 2)
+    send_second(cx, y, r2x, REST, 1, 2)
+    add_first(by, y, r1y, cy, REST, 1, 2)
+    send_second(cy, x, r2y, REST, 0, 2)
+    add_second(cx, y, r2x, 0, NEXT, 1, 1)
+    add_second(cy, x, r2y, 8, NEXT, 0, 1)
+    for plane in range(4, 8):
+        send_z(plane)
+    add_second(cx, y, r2x, 0, REST, 1, 2)
+    add_second(cy, x, r2y, 8, REST, 0, 2)
+    for plane in PLANES_REST:
+        send_z(plane)
 
     arrived(r3.at[pl.ds(1, 15)], z_rs.at[0])
-    acc = dz[slot(z)].astype(F32)
+    acc = dz[8 * lax.rem(z, 2) + z // 2].astype(F32)
     for d in range(1, 16):
         acc = acc + r3[d].astype(F32)
 
     piece[...] = (acc * (1.0 / LOSS_SCALE)).astype(BF16)
-    home_slot = 2 * lax.rem(z + target, 8) + core
-    gath[home_slot] = piece[...]
+    gath[slide] = piece[...]
     for o in SLIDE_ORDER:
         dy, dx, dc = o // 4, (o // 2) % 2, o % 2
         xl = lax.rem(x_lo + dx, 2)
         cc = lax.rem(core + dc, 2)
         pltpu.make_async_remote_copy(
-            src_ref=piece, dst_ref=gath.at[home_slot], send_sem=ag_ss.at[0],
+            src_ref=piece, dst_ref=gath.at[slide], send_sem=ag_ss.at[0],
             recv_sem=ag_rs.at[0], device_id=dev(2 * x_hi + xl, lax.rem(y + dy, 4), z, cc),
             device_id_type=MESH,
         ).start()
@@ -449,8 +462,8 @@
             vm((4, 8, 16, 128), BF16), vm((4, 8, 16, 128), BF16),
             vm((3, 8, 16, 128), BF16), vm((3, 8, 16, 128), BF16),
             vm((16, 16, 128), BF16), vm((16, 16, 128), BF16),
-            dma((6,)), dma((1,)), dma((2,)), dma((1,)), dma((2,)), dma((2,)), dma((4,)),
-            dma((2,)), dma((4,)), dma((1,)), dma((1,)), dma((1,)), dma((1,)),
+            dma((6,)), dma((1,)), dma((2,)), dma((1,)), dma((2,)), dma((2,)), dma((6,)),
+            dma((2,)), dma((6,)), dma((1,)), dma((1,)), dma((1,)), dma((1,)),
             pltpu.SemaphoreType.REGULAR,
         ],
         compiler_params=pltpu.CompilerParams(

time: 46.7 us -> 42.8 us (0.916)
  Pallas kernels: 45.9 us -> 42 us
    pallas_call x1, Pallas kernels: 45.1 us -> 41.2 us  [local(): pl.pallas_call(kernel, out_shape=(vm((256, 512), BF16), vm((64, 1024), BF...]
where the time goes in v4:
time: 42.8 us; the launch traced here: 42.6 us
  Pallas kernels  42 us (98%)
  between operations  0.65 us (2%)
    pallas_call x1, Pallas kernels, local(): pl.pallas_call(kernel, out_shape=(vm((256, 512), BF16), vm((64, 1024), BF...  41.2 us

profile of v4, /device:TPU:1, one launch (start us, length us, event | category | flops | bytes accessed | tf_op | source)
XLA Modules:
  0.0 42.6 jit_solution(8862690208806245210)
XLA Ops:
  0.6 41.2 %pyramid_backward.1 = (bf16[256,512]{1,0:T(8,128)(2,1)S(1)}, bf16[64,1024]{1,0:T(8,128)(2,1)S(1)}, bf16[16,16,128]{2,1,0:T(8,128)(2,1)S(1)}) custom-call(bf16[256,512]{1,0:T(8,128)(2,1)} %bitcast.14, bf16[64,1024]{1,0:T(8,128)(2,1)} %bitcast.15, bf16[256,256]{1,0:T(8,128)(2,1)} %bitcast.16, bf16[64,256]{1,0:T(8,128)(2,1)} %bitcast.19, ...), custom_call_target="tpu_custom_call" | custom-call | tf_op jit(solution)/shard_map/pyramid_backward/pallas_call | solution.py:444
  41.8 0.8 %place_outputs.1 = (bf16[256,512]{1,0:T(8,128)(2,1)}, bf16[64,1024]{1,0:T(8,128)(2,1)}, f32[72,256]{1,0:T(8,128)}, f32[8]{0:T(128)}, f32[16,256]{1,0:T(8,128)}, /*index=5*/f32[32,256]{1,0:T(8,128)}) custom-call(bf16[256,512]{1,0:T(8,128)(2,1)S(1)} %get-tuple-element.15.t3, bf16[64,1024]{1,0:T(8,128)(2,1)S(1)} %get-tuple-element.16.t4, ...), custom_call_target="tpu_custom_call" | custom-call | tf_op jit(solution)/shard_map/place_outputs/pallas_call | solution.py:474

commit v5 on v4

--- a/solution.py
+++ b/solution.py
@@ -14,7 +14,11 @@
 ROW_C3 = 2320
 ROW_C4 = 2832
 ROWS = 3856
-AHEAD, NEXT, REST = (0, 2), (2, 2), (4, 4)
+NEXT, REST = (0, 2), (2, 4)
+PLANE_STEPS = (
+    (2, 2), (2, 1), (2, 3), (1, 2), (3, 2), (2, 0), (0, 2), (1, 1), (1, 3), (3, 1), (3, 3),
+    (1, 0), (3, 0), (0, 1), (0, 3),
+)
 C3_AHEAD, C4_AHEAD = 128, 256
 ROWS_AHEAD = 768 + 16 + C3_AHEAD + C4_AHEAD
 P3, G3, P4, G4, F3, F4, HW, L3, L4, WIDE = 0, 256, 512, 576, 640, 896, 960, 3264, 3776, 4800
@@ -35,8 +39,8 @@
     t3, t4, gath,
     piece, wide, tc3, tc4, k3, k4,
     f3t, f4t, c3t, c4t, edge_t, dx3, dx4, halo_s, halo_r, part, back_s, early, grads,
-    core_s, core_r, bx, by, r1x, r1y, cx, cy, r2x, r2y, dz, r3,
-    in_sem, halo_ss, halo_rs, core_ss, core_rs, s1_ss, s1_rs, s2_ss, s2_rs,
+    core_s, core_r, ahead_s, ahead_r, bx, by, r1x, r1y, cx, cy, r2x, r2y, dz, r3,
+    in_sem, halo_ss, halo_rs, core_ss, core_rs, ahead_ss, ahead_rs, s1_ss, s1_rs, s2_ss, s2_rs,
     z_ss, z_rs, ag_ss, ag_rs, far_sem,
 ):
     slide = lax.axis_index("slide")
@@ -72,6 +76,10 @@
     barrier = pltpu.get_barrier_semaphore()
     partners = [above, below]
     partners += [z_dev(d) for d in (-4, 4, -3, 3, -2, 2, -1, 1)] + x_dev + y_dev + [sibling]
+    plane_dev = [
+        dev(lax.rem(x + i, 4), lax.rem(y + j, 4), z, core) for i, j in PLANE_STEPS
+    ]
+    partners += [who for who, (i, j) in zip(plane_dev, PLANE_STEPS) if i and j]
     load_wide(p3_h, P3, 256, 0)
     load_wide(g3_h, G3, 256, 0)
     load_wide(p4_h, P4, 64, 0)
@@ -255,27 +263,26 @@
     def block(at):
         return grads[at : at + 16, :] + core_r[at : at + 16, :].astype(F32)
 
-    def pack(half, places):
+    def placed(xx, yy, plane):
+        xh, xl = xx // 2, xx % 2
+        kind, r = 2 * yy + xl, 2 * plane + xh
+        if kind < 4:
+            val = block(144 * plane + 80 * xh + 16 * kind)
+        elif kind == 4:
+            split = block(144 * plane + 64)
+            val = jnp.concatenate([split[8 * xh : 8 * xh + 8], bias_rows], axis=0)
+        elif kind == 5:
+            val = block(ROW_C3 + 16 * r)
+        else:
+            val = block(ROW_C4 + 32 * r + 16 * (kind - 6))
+        return val.astype(BF16)
+
+    def pack(places):
         for xx in range(4):
-            xh, xl = xx // 2, xx % 2
             for yy in range(4):
-                kind = 2 * yy + xl
                 for place in range(places[0], places[0] + places[1]):
-                    plane = 2 * place + half
-                    r = 2 * plane + xh
-                    if kind < 4:
-                        val = block(144 * plane + 80 * xh + 16 * kind)
-                    elif kind == 4:
-                        split = block(144 * plane + 64)
-                        val = jnp.concatenate([split[8 * xh : 8 * xh + 8], bias_rows], axis=0)
-                    elif kind == 5:
-                        val = block(ROW_C3 + 16 * r)
-                    else:
-                        val = block(ROW_C4 + 32 * r + 16 * (kind - 6))
-                    if half:
-                        by[yy, place, xx] = val.astype(BF16)
-                    else:
-                        bx[xx, place, yy] = val.astype(BF16)
+                    bx[xx, place, yy] = placed(xx, yy, 2 * place + 4)
+                    by[yy, place, xx] = placed(xx, yy, 2 * place + 5)
 
     def arrived(ref, sem):
         pltpu.make_async_copy(ref, ref, sem).wait()
@@ -285,7 +292,7 @@
         for d in (2, 1, 3):
             pltpu.make_async_remote_copy(
                 src_ref=src.at[lax.rem(at + d, 4), blocks], dst_ref=dst.at[d - 1, blocks],
-                send_sem=s1_ss.at[axis], recv_sem=s1_rs.at[3 * axis + group],
+                send_sem=s1_ss.at[axis], recv_sem=s1_rs.at[2 * axis + group],
                 device_id=(x_dev, y_dev)[axis][d - 1], device_id_type=MESH,
             ).start()
 
@@ -294,12 +301,12 @@
         for d in (2, 1, 3):
             pltpu.make_async_remote_copy(
                 src_ref=src.at[lax.rem(at + d, 4), blocks], dst_ref=dst.at[d - 1, blocks],
-                send_sem=s2_ss.at[axis], recv_sem=s2_rs.at[3 * axis + group],
+                send_sem=s2_ss.at[axis], recv_sem=s2_rs.at[2 * axis + group],
                 device_id=(x_dev, y_dev)[axis][d - 1], device_id_type=MESH,
             ).start()
 
     def add_first(src, at, got, out, places, axis, group):
-        arrived(got.at[:, pl.ds(*places)], s1_rs.at[3 * axis + group])
+        arrived(got.at[:, pl.ds(*places)], s1_rs.at[2 * axis + group])
         for k in range(places[0], places[0] + places[1]):
             acc = src[at, k].astype(F32)
             for d in range(3):
@@ -308,7 +315,7 @@
                 out[i, k] = acc[i].astype(BF16)
 
     def add_second(src, at, got, base, places, axis, group):
-        arrived(got.at[:, pl.ds(*places)], s2_rs.at[3 * axis + group])
+        arrived(got.at[:, pl.ds(*places)], s2_rs.at[2 * axis + group])
         lo, n = places
         acc = src[at, lo : lo + n].astype(F32)
         for d in range(3):
@@ -317,27 +324,31 @@
 
     arrived(core_r.at[pl.ds(0, ROWS_AHEAD)], core_rs.at[0])
     bias_rows = block(ROW_BIAS)[0:8]
-    pack(0, AHEAD)
-    send_first(bx, x, r1x, AHEAD, 0, 0)
-    pack(1, AHEAD)
-    send_first(by, y, r1y, AHEAD, 1, 0)
+    for xx in range(4):
+        for yy in range(4):
+            for plane in range(4):
+                ahead_s[xx, yy, plane] = placed(xx, yy, plane)
+    for i, (dx, dy) in enumerate(PLANE_STEPS):
+        pltpu.make_async_remote_copy(
+            src_ref=ahead_s.at[lax.rem(x + dx, 4), lax.rem(y + dy, 4)],
+            dst_ref=ahead_r.at[i], send_sem=ahead_ss.at[0], recv_sem=ahead_rs.at[0],
+            device_id=plane_dev[i], device_id_type=MESH,
+        ).start()
 
     arrived(core_r.at[pl.ds(0, ROWS - ROWS_AHEAD)], core_rs.at[1])
     for places in (NEXT, REST):
-        pack(0, places)
-        pack(1, places)
+        pack(places)
     t3[0:32, :] = nt(lat3[0:32], l3).astype(BF16)
     t3[224:256, :] = nt(lat3[224:256], l3).astype(BF16)
     t4[...] = nt(lat4, l4).astype(BF16)
 
-    add_first(bx, x, r1x, cx, AHEAD, 0, 0)
-    send_second(cx, y, r2x, AHEAD, 1, 0)
-    add_first(by, y, r1y, cy, AHEAD, 1, 0)
-    send_second(cy, x, r2y, AHEAD, 0, 0)
-    send_first(bx, x, r1x, NEXT, 0, 1)
-    send_first(by, y, r1y, NEXT, 1, 1)
-    send_first(bx, x, r1x, REST, 0, 2)
-    send_first(by, y, r1y, REST, 1, 2)
+    send_first(bx, x, r1x, NEXT, 0, 0)
+    send_first(by, y, r1y, NEXT, 1, 0)
+    send_first(bx, x, r1x, REST, 0, 1)
+    send_first(by, y, r1y, REST, 1, 1)
+
+    def slot(plane):
+        return plane if plane < 4 else 4 + 6 * (plane % 2) + (plane - 4) // 2
 
     def send_z(plane):
         d = lax.rem(plane - z + 16, 16)
@@ -345,52 +356,68 @@
         @pl.when(d != 0)
         def _():
             pltpu.make_async_remote_copy(
-                src_ref=dz.at[8 * (plane % 2) + plane // 2], dst_ref=r3.at[d],
+                src_ref=dz.at[slot(plane)], dst_ref=r3.at[d],
                 send_sem=z_ss.at[0], recv_sem=z_rs.at[0], device_id=dev(x, y, plane, core),
                 device_id_type=MESH,
             ).start()
 
-    add_second(cx, y, r2x, 0, AHEAD, 1, 0)
-    add_second(cy, x, r2y, 8, AHEAD, 0, 0)
+    arrived(ahead_r, ahead_rs.at[0])
+    for plane in range(4):
+        acc = ahead_s[x, y, plane].astype(F32)
+        for i in range(15):
+            acc = acc + ahead_r[i, plane].astype(F32)
+        dz[plane] = acc.astype(BF16)
     pl.semaphore_wait(far_sem, 2)
     for plane in range(4):
         send_z(plane)
-    add_first(bx, x, r1x, cx, NEXT, 0, 1)
-    send_second(cx, y, r2x, NEXT, 1, 1)
-    add_first(by, y, r1y, cy, NEXT, 1, 1)
-    send_second(cy, x, r2y, NEXT, 0, 1)
-    add_first(bx, x, r1x, cx, REST, 0, 2)
-    send_second(cx, y, r2x, REST, 1, 2)
-    add_first(by, y, r1y, cy, REST, 1, 2)
-    send_second(cy, x, r2y, REST, 0, 2)
-    add_second(cx, y, r2x, 0, NEXT, 1, 1)
-    add_second(cy, x, r2y, 8, NEXT, 0, 1)
+    add_first(bx, x, r1x, cx, NEXT, 0, 0)
+    send_second(cx, y, r2x, NEXT, 1, 0)
+    add_first(by, y, r1y, cy, NEXT, 1, 0)
+    send_second(cy, x, r2y, NEXT, 0, 0)
+    add_first(bx, x, r1x, cx, REST, 0, 1)
+    send_second(cx, y, r2x, REST, 1, 1)
+    add_first(by, y, r1y, cy, REST, 1, 1)
+    send_second(cy, x, r2y, REST, 0, 1)
+    add_second(cx, y, r2x, 4, NEXT, 1, 0)
+    add_second(cy, x, r2y, 10, NEXT, 0, 0)
     for plane in range(4, 8):
         send_z(plane)
-    add_second(cx, y, r2x, 0, REST, 1, 2)
-    add_second(cy, x, r2y, 8, REST, 0, 2)
+    def finish_plane():
+        arrived(r3.at[pl.ds(1, 15)], z_rs.at[0])
+        high = (z + 12) // 16
+        home = (1 - high) * z + high * (4 + 6 * lax.rem(z, 2) + (z + 12) // 2 - 8)
+        acc = dz[home].astype(F32)
+        for d in range(1, 16):
+            acc = acc + r3[d].astype(F32)
+
+        piece[...] = (acc * (1.0 / LOSS_SCALE)).astype(BF16)
+        gath[slide] = piece[...]
+        for o in SLIDE_ORDER:
+            dy, dx, dc = o // 4, (o // 2) % 2, o % 2
+            xl = lax.rem(x_lo + dx, 2)
+            cc = lax.rem(core + dc, 2)
+            pltpu.make_async_remote_copy(
+                src_ref=piece, dst_ref=gath.at[slide], send_sem=ag_ss.at[0],
+                recv_sem=ag_rs.at[0], device_id=dev(2 * x_hi + xl, lax.rem(y + dy, 4), z, cc),
+                device_id_type=MESH,
+            ).start()
+
+    @pl.when(z < 2)
+    def _():
+        finish_plane()
+
+    add_second(cx, y, r2x, 4, REST, 1, 1)
+    add_second(cy, x, r2y, 10, REST, 0, 1)
     for plane in PLANES_REST:
         send_z(plane)
 
-    arrived(r3.at[pl.ds(1, 15)], z_rs.at[0])
-    acc = dz[8 * lax.rem(z, 2) + z // 2].astype(F32)
-    for d in range(1, 16):
-        acc = acc + r3[d].astype(F32)
-
-    piece[...] = (acc * (1.0 / LOSS_SCALE)).astype(BF16)
-    gath[slide] = piece[...]
-    for o in SLIDE_ORDER:
-        dy, dx, dc = o // 4, (o // 2) % 2, o % 2
-        xl = lax.rem(x_lo + dx, 2)
-        cc = lax.rem(core + dc, 2)
-        pltpu.make_async_remote_copy(
-            src_ref=piece, dst_ref=gath.at[slide], send_sem=ag_ss.at[0],
-            recv_sem=ag_rs.at[0], device_id=dev(2 * x_hi + xl, lax.rem(y + dy, 4), z, cc),
-            device_id_type=MESH,
-        ).start()
+    @pl.when(z >= 2)
+    def _():
+        finish_plane()
 
     arrived(halo_s, halo_ss.at[0])
     arrived(core_s, core_ss.at[0])
+    arrived(ahead_r, ahead_ss.at[0])
     for axis in range(2):
         arrived(bx.at[pl.ds(0, 3)], s1_ss.at[axis])
         arrived(cx.at[pl.ds(0, 3)], s2_ss.at[axis])
@@ -457,13 +484,14 @@
             vm((2, 48, 256), BF16), vm((2, 48, 256), BF16),
             vm((1536, 256), F32), vm((320, 256), F32), vm((512, 256), F32),
             vm((ROWS, 128), F32), vm((ROWS, 128), BF16), vm((ROWS, 128), BF16),
-            vm((4, 8, 4, 16, 128), BF16), vm((4, 8, 4, 16, 128), BF16),
-            vm((3, 8, 4, 16, 128), BF16), vm((3, 8, 4, 16, 128), BF16),
-            vm((4, 8, 16, 128), BF16), vm((4, 8, 16, 128), BF16),
-            vm((3, 8, 16, 128), BF16), vm((3, 8, 16, 128), BF16),
+            vm((4, 4, 4, 16, 128), BF16), vm((15, 4, 16, 128), BF16),
+            vm((4, 6, 4, 16, 128), BF16), vm((4, 6, 4, 16, 128), BF16),
+            vm((3, 6, 4, 16, 128), BF16), vm((3, 6, 4, 16, 128), BF16),
+            vm((4, 6, 16, 128), BF16), vm((4, 6, 16, 128), BF16),
+            vm((3, 6, 16, 128), BF16), vm((3, 6, 16, 128), BF16),
             vm((16, 16, 128), BF16), vm((16, 16, 128), BF16),
-            dma((6,)), dma((1,)), dma((2,)), dma((1,)), dma((2,)), dma((2,)), dma((6,)),
-            dma((2,)), dma((6,)), dma((1,)), dma((1,)), dma((1,)), dma((1,)),
+            dma((6,)), dma((1,)), dma((2,)), dma((1,)), dma((2,)), dma((1,)), dma((1,)),
+            dma((2,)), dma((4,)), dma((2,)), dma((4,)), dma((1,)), dma((1,)), dma((1,)), dma((1,)),
             pltpu.SemaphoreType.REGULAR,
         ],
         compiler_params=pltpu.CompilerParams(

time: 42.8 us -> 41.1 us (0.960)
  Pallas kernels: 42 us -> 40.3 us
    pallas_call x1, Pallas kernels: 41.2 us -> 39.5 us  [local(): pl.pallas_call(kernel, out_shape=(vm((256, 512), BF16), vm((64, 1024), BF...]
where the time goes in v5:
time: 41.1 us; the launch traced here: 40.9 us
  Pallas kernels  40.3 us (98%)
  between operations  0.65 us (2%)
    pallas_call x1, Pallas kernels, local(): pl.pallas_call(kernel, out_shape=(vm((256, 512), BF16), vm((64, 1024), BF...  39.5 us
    pallas_call x1, Pallas kernels, local(): pl.pallas_call(finish, out_shape=(jax.ShapeDtypeStruct((256, 512), BF16),...  0.83 us

profile of v5, /device:TPU:1, one launch (start us, length us, event | category | flops | bytes accessed | tf_op | source)
XLA Modules:
  0.0 40.9 jit_solution(15385229382106401690)
XLA Ops:
  0.6 39.5 %pyramid_backward.1 = (bf16[256,512]{1,0:T(8,128)(2,1)S(1)}, bf16[64,1024]{1,0:T(8,128)(2,1)S(1)}, bf16[16,16,128]{2,1,0:T(8,128)(2,1)S(1)}) custom-call(bf16[256,512]{1,0:T(8,128)(2,1)} %bitcast.14, bf16[64,1024]{1,0:T(8,128)(2,1)} %bitcast.15, bf16[256,256]{1,0:T(8,128)(2,1)} %bitcast.16, bf16[64,256]{1,0:T(8,128)(2,1)} %bitcast.19, ...), custom_call_target="tpu_custom_call" | custom-call | tf_op jit(solution)/shard_map/pyramid_backward/pallas_call | solution.py:471
  40.1 0.8 %place_outputs.1 = (bf16[256,512]{1,0:T(8,128)(2,1)}, bf16[64,1024]{1,0:T(8,128)(2,1)}, f32[72,256]{1,0:T(8,128)}, f32[8]{0:T(128)}, f32[16,256]{1,0:T(8,128)}, /*index=5*/f32[32,256]{1,0:T(8,128)}) custom-call(bf16[256,512]{1,0:T(8,128)(2,1)S(1)} %get-tuple-element.15.t3, bf16[64,1024]{1,0:T(8,128)(2,1)S(1)} %get-tuple-element.16.t4, ...), custom_call_target="tpu_custom_call" | custom-call | tf_op jit(solution)/shard_map/place_outputs/pallas_call | solution.py:502

commit v6 on v5

--- a/solution.py
+++ b/solution.py
@@ -195,11 +195,13 @@
     l3, l4 = wide[L3 : L3 + 512, :], wide[L4 : L4 + 1024, :]
     t3[32:224, :] = nt(inner, l3).astype(BF16)
 
-    def edge_side(side):
+    def edge_wait(side):
         pltpu.make_async_remote_copy(
             src_ref=halo_s.at[side], dst_ref=halo_r.at[side], send_sem=halo_ss.at[0],
             recv_sem=halo_rs.at[side], device_id=above, device_id_type=MESH,
         ).wait_recv()
+
+    def edge_rows(side):
         valid = row > 0 if side else row < 31
         val = jnp.where(valid, halo_r[side].astype(F32), 0.0)
         i = lax.broadcasted_iota(jnp.int32, (48, 256), 0)
@@ -224,12 +226,24 @@
             val = part[at : at + 256, :] + nn(edge_t[1 - side], shifted[b])
             emit(1536 * side + 256 * b, 256, val)
 
-    low = edge_side(0)
+    def above_back():
+        edge_wait(1)
+        edge_back(1, edge_rows(1))
+
+    @pl.when(x_hi == 1)
+    def _():
+        above_back()
+
+    edge_wait(0)
+    low = edge_rows(0)
     edge_head(0, low)
     core_copy(0, 768, 0).start()
     edge_back(0, low)
-    top = edge_side(1)
-    edge_back(1, top)
+
+    @pl.when(x_hi == 0)
+    def _():
+        above_back()
+
 
     back3 = back_s[0:256, :]
     lat3 = back3.astype(BF16)
@@ -253,7 +267,7 @@
     core_copy(ROW_BIAS, 16 + C3_AHEAD, 0).start()
     emit_c4(0, C4_AHEAD)
     core_copy(ROW_C4, C4_AHEAD, 0).start()
-    edge_head(1, top)
+    edge_head(1, edge_rows(1))
     core_copy(1536, 768, 1).start()
     emit_c3(C3_AHEAD, 512)
     core_copy(ROW_C3 + C3_AHEAD, 512 - C3_AHEAD, 1).start()
@@ -402,7 +416,7 @@
                 device_id_type=MESH,
             ).start()
 
-    @pl.when(z < 2)
+    @pl.when(z < 4)
     def _():
         finish_plane()
 
@@ -411,7 +425,7 @@
     for plane in PLANES_REST:
         send_z(plane)
 
-    @pl.when(z >= 2)
+    @pl.when(z >= 4)
     def _():
         finish_plane()
 

time: 41.1 us -> 40.8 us (level)
  no operation moved by 1% of the time
where the time goes in v6:
time: 40.8 us; the launch traced here: 40.7 us
  Pallas kernels  40 us (98%)
  between operations  0.65 us (2%)
    pallas_call x1, Pallas kernels, local(): pl.pallas_call(kernel, out_shape=(vm((256, 512), BF16), vm((64, 1024), BF...  39.2 us
    pallas_call x1, Pallas kernels, local(): pl.pallas_call(finish, out_shape=(jax.ShapeDtypeStruct((256, 512), BF16),...  0.83 us

profile of v6, /device:TPU:1, one launch (start us, length us, event | category | flops | bytes accessed | tf_op | source)
XLA Modules:
  0.0 40.7 jit_solution(13873960851213531932)
XLA Ops:
  0.6 39.2 %pyramid_backward.1 = (bf16[256,512]{1,0:T(8,128)(2,1)S(1)}, bf16[64,1024]{1,0:T(8,128)(2,1)S(1)}, bf16[16,16,128]{2,1,0:T(8,128)(2,1)S(1)}) custom-call(bf16[256,512]{1,0:T(8,128)(2,1)} %bitcast.14, bf16[64,1024]{1,0:T(8,128)(2,1)} %bitcast.15, bf16[256,256]{1,0:T(8,128)(2,1)} %bitcast.16, bf16[64,256]{1,0:T(8,128)(2,1)} %bitcast.19, ...), custom_call_target="tpu_custom_call" | custom-call | tf_op jit(solution)/shard_map/pyramid_backward/pallas_call | solution.py:485
  39.8 0.8 %place_outputs.1 = (bf16[256,512]{1,0:T(8,128)(2,1)}, bf16[64,1024]{1,0:T(8,128)(2,1)}, f32[72,256]{1,0:T(8,128)}, f32[8]{0:T(128)}, f32[16,256]{1,0:T(8,128)}, /*index=5*/f32[32,256]{1,0:T(8,128)}) custom-call(bf16[256,512]{1,0:T(8,128)(2,1)S(1)} %get-tuple-element.15.t3, bf16[64,1024]{1,0:T(8,128)(2,1)S(1)} %get-tuple-element.16.t4, ...), custom_call_target="tpu_custom_call" | custom-call | tf_op jit(solution)/shard_map/place_outputs/pallas_call | solution.py:516
